TPU v7x, 32 devices: a whole 2x2x4 slice. The times are simulated.
32 devices in a mesh: grp: 4 (over x, core), seq: 8 (over z, y).
Axes of the slice: x: 2, y: 2, z: 4, core: 2. Of those that a mesh axis runs over, the one named last changes fastest.
Arguments:
- tokens: bfloat16 [4096, 2048], P(('grp', 'seq')), may hold values from -6 to 6
- doc_lengths: int32 [4, 8], P('grp'), may hold values from 1 to 897, 1024 in all within a row
- cotangent: bfloat16 [4096, 2048], P(('grp', 'seq')), may hold values from -6 to 6
- attn_gain: bfloat16 [2048], P(('grp', 'seq')), may hold values from 0.5 to 1.5
- query_weight: bfloat16 [2048, 1024], P(('grp', 'seq')), may hold values from -0.125 to 0.125
- key_weight: bfloat16 [2048, 1024], P(('grp', 'seq')), may hold values from -0.125 to 0.125
- value_weight: bfloat16 [2048, 2048], P(('grp', 'seq')), may hold values from -0.125 to 0.125
- gate_weight: bfloat16 [2048, 2048], P(('grp', 'seq')), may hold values from -0.125 to 0.125
- rank_in: bfloat16 [2048, 16], P(('grp', 'seq')), may hold values from -0.125 to 0.125
- rank_out: bfloat16 [1024, 16], P(('grp', 'seq')), may hold values from -3 to 3
- decay_bias: bfloat16 [1024], P(('grp', 'seq')), may hold values from -1 to 12, as said below
- head_gain: bfloat16 [512], P(('grp', 'seq')), may hold values from 0.5 to 1.5
- out_weight: bfloat16 [2048, 2048], P(('grp', 'seq')), may hold values from -0.25 to 0.25
- mlp_gain: bfloat16 [2048], P(('grp', 'seq')), may hold values from 0.5 to 1.5
- mlp_gate_weight: bfloat16 [2048, 5632], P(('grp', 'seq')), may hold values from -0.125 to 0.125
- mlp_up_weight: bfloat16 [2048, 5632], P(('grp', 'seq')), may hold values from -0.125 to 0.125
- down_weight: bfloat16 [2048, 5632], P(('grp', 'seq')), may hold values from -0.109375 to 0.109375
Outputs:
- layer_out: float32 [4096, 2048], P(('grp', 'seq'))
- tokens_grad: float32 [4096, 2048], P(('grp', 'seq'))
- attn_gain_grad: float32 [2048], P(('grp', 'seq'))
- query_grad: float32 [2048, 1024], P(('grp', 'seq'))
- key_grad: float32 [2048, 1024], P(('grp', 'seq'))
- value_grad: float32 [2048, 2048], P(('grp', 'seq'))
- gate_grad: float32 [2048, 2048], P(('grp', 'seq'))
- rank_in_grad: float32 [2048, 16], P(('grp', 'seq'))
- rank_out_grad: float32 [1024, 16], P(('grp', 'seq'))
- decay_bias_grad: float32 [1024], P(('grp', 'seq'))
- head_gain_grad: float32 [512], P(('grp', 'seq'))
- out_weight_grad: float32 [2048, 2048], P(('grp', 'seq'))
- mlp_gain_grad: float32 [2048], P(('grp', 'seq'))
- mlp_gate_grad: float32 [2048, 5632], P(('grp', 'seq'))
- mlp_up_grad: float32 [2048, 5632], P(('grp', 'seq'))
- down_grad: float32 [2048, 5632], P(('grp', 'seq'))
Inputs may be any that keep to these rules, and one draw needn't show every extreme that they name: `doc_lengths`: row s lists the lengths of the 8 documents packed, in order, into sequence s; they sum to 1024, and one of them is 897. `decay_bias`: one bias a key channel.
All inputs are finite; a program needn't handle non-finite values.
Results may differ from a plain program's by a relative error of at most 0.035.
Values may be sent and summed in bfloat16 or wider, within the bound.
A program may use at most 576 MiB of HBM per device.

v0:
```python
import functools

import jax
import jax.numpy as jnp
import numpy as np
from jax import lax
from jax.experimental import pallas as pl
from jax.experimental.pallas import tpu as pltpu
from jax.sharding import Mesh
from jax.sharding import PartitionSpec as P

H = 4
DK = 256
DV = 512
R = 16
CHUNK = 128
LEVELS = 7
SMALL = 128
RANK_AT = 32
HEAD_AT = 64
WAIT_FLOPS = 100_000_000
LANES = 128
TILE = 256
PIECES = 2
norm_eps = 1e-06
head_eps = 0.25
decay_norm = 16.0
BF = jnp.bfloat16
F32 = jnp.float32
REST = ("x", "c", "y")
OWN = ("x", "c", "z", "y")


def dot_plain(left, right):
    return jnp.dot(left, right, preferred_element_type=F32)


def dot_rows(left, right):
    return lax.dot_general(left, right, (((1,), (1,)), ((), ())), preferred_element_type=F32)


def dot_cols(left, right):
    return lax.dot_general(left, right, (((0,), (0,)), ((), ())), preferred_element_type=F32)


def split_two(value):
    high = value.astype(BF)
    return jnp.concatenate([high, (value - high.astype(F32)).astype(BF)], axis=1)


def sum_two(value):
    half = value.shape[1] // 2
    return value[:, :half] + value[:, half:]


def chunk_tables():
    t = np.arange(CHUNK)[:, None]
    j = np.arange(CHUNK)[None, :]
    parts = []
    level = np.full((CHUNK, CHUNK), -1, np.int32)
    for number in range(LEVELS):
        half = CHUNK >> (number + 1)
        middle = t // (2 * half) * (2 * half) + half - 1
        upper = t % (2 * half) >= half
        parts.append(np.where(upper, (j > middle) & (j <= t), (j > t) & (j <= middle)))
        pair = (t // (2 * half) == j // (2 * half)) & upper & (j % (2 * half) < half)
        level[pair] = number
    level[np.arange(CHUNK), np.arange(CHUNK)] = LEVELS
    parts.append(j <= t)
    parts.append(j > t)
    return np.concatenate(parts, axis=0).astype(np.float32), level


def upper_rows(number):
    half = CHUNK >> (number + 1)
    rows = lax.broadcasted_iota(jnp.int32, (CHUNK, 1), 0)
    return lax.rem(rows, 2 * half) >= half


def factors(ld_ref, sums_ref):
    exponents = sum_two(dot_plain(sums_ref[...], split_two(ld_ref[...])))
    return jnp.exp(exponents)


def rows_of(value, number):
    return value[number * CHUNK : (number + 1) * CHUNK]


def mix_forward_body(
    q_ref, k_ref, v_ref, ld_ref, aux_ref, seg_ref, sums_ref, level_ref,
    out_ref, enter_ref, score_ref, state,
):
    @pl.when(pl.program_id(0) == 0)
    def _():
        state[...] = jnp.zeros_like(state)

    factor = factors(ld_ref, sums_ref)
    query = q_ref[...].astype(F32) * DK ** (-0.5)
    key = k_ref[...].astype(F32)
    level = level_ref[...]
    aux = aux_ref[...]
    scores = jnp.where(level == LEVELS, dot_rows(query.astype(BF), k_ref[...]), 0.0)
    for number in range(LEVELS):
        part = rows_of(factor, number)
        pairs = dot_rows((query * part).astype(BF), (key * part).astype(BF))
        scores = jnp.where(level == number, pairs, scores)
    scores = jnp.where(aux[:, 2:3] == seg_ref[0], scores, 0.0).astype(BF)
    score_ref[0] = scores
    cumulative = rows_of(factor, LEVELS)
    enter = state[...].astype(BF)
    enter_ref[0] = enter
    lifted = (query * cumulative * aux[:, 0:1]).astype(BF)
    ending = (key * rows_of(factor, LEVELS + 1) * aux[:, 1:2]).astype(BF)
    out = dot_plain(scores, v_ref[...]) + dot_rows(lifted, enter)
    out_ref[...] = out.astype(out_ref.dtype)
    through = cumulative[CHUNK - 1 :] * aux[0:1, 3:4]
    state[...] = state[...] * through + dot_cols(v_ref[...], ending)


def mix_backward_body(
    q_ref, k_ref, v_ref, ld_ref, aux_ref, seg_ref, sums_ref, sums_t_ref, level_ref, level_t_ref,
    enter_ref, score_ref, do_ref,
    dq_ref, dk_ref, dv_ref, dld_ref, state,
):
    @pl.when(pl.program_id(0) == 0)
    def _():
        state[...] = jnp.zeros_like(state)

    factor = factors(ld_ref, sums_ref)
    scale = DK ** (-0.5)
    query = q_ref[...].astype(F32) * scale
    key = k_ref[...].astype(F32)
    value = v_ref[...]
    grad = do_ref[...]
    level = level_ref[...]
    level_t = level_t_ref[...]
    aux = aux_ref[...]
    same = aux[:, 2:3] == seg_ref[0]
    weight = jnp.where(same, dot_rows(grad, value), 0.0)
    weight_t = jnp.where(same, dot_rows(value, grad), 0.0)
    diagonal = jnp.sum(jnp.where(level == LEVELS, weight, 0.0), axis=1, keepdims=True)
    dq = diagonal * key
    dk = diagonal * query
    moved = []
    for number in range(LEVELS):
        part = rows_of(factor, number)
        left = jnp.concatenate(
            [
                jnp.where(level == number, weight, 0.0).astype(BF),
                jnp.where(level_t == number, weight_t, 0.0).astype(BF),
            ],
            axis=1,
        )
        right = jnp.concatenate([(key * part).astype(BF), (query * part).astype(BF)], axis=0)
        both = dot_plain(left, right) * part
        upper = upper_rows(number)
        dq = dq + jnp.where(upper, both, 0.0)
        dk = dk + jnp.where(upper, 0.0, both)
        moved.append(both * jnp.where(upper, query, key))
    cumulative = rows_of(factor, LEVELS)
    enter = enter_ref[0]
    after = state[...]
    after_low = after.astype(BF)
    lift = cumulative * aux[:, 0:1]
    finish = rows_of(factor, LEVELS + 1) * aux[:, 1:2]
    lifted = query * lift
    ending = key * finish
    from_enter = dot_plain(grad, enter)
    from_after = dot_plain(value, after_low)
    moved.append(lifted * from_enter)
    moved.append(ending * from_after)
    dq_ref[...] = ((dq + lift * from_enter) * scale).astype(dq_ref.dtype)
    dk_ref[...] = (dk + finish * from_after).astype(dk_ref.dtype)
    dv = dot_cols(score_ref[0], grad) + dot_rows(ending.astype(BF), after_low)
    dv_ref[...] = dv.astype(dv_ref.dtype)
    through = cumulative[CHUNK - 1 :] * aux[0:1, 3:4]
    passing = jnp.sum(after * enter.astype(F32), axis=0, keepdims=True) * through
    spread = sum_two(dot_plain(sums_t_ref[...], split_two(jnp.concatenate(moved, axis=0))))
    dld_ref[...] = spread + passing
    state[...] = after * through + dot_cols(grad, lifted.astype(BF))


def mix_specs(count, width, backward):
    def at(i):
        return count - 1 - i if backward else i

    def tokens(columns):
        return pl.BlockSpec((CHUNK, columns), lambda i: (at(i), 0))

    def chunks(rows, columns):
        return pl.BlockSpec((1, rows, columns), lambda i: (at(i), 0, 0))

    def whole(rows, columns):
        return pl.BlockSpec((rows, columns), lambda i: (0, 0))

    return tokens, chunks, whole


def mix_forward(query, key, value, log_decay, aux, seg_rows):
    total, width = value.shape
    count = total // CHUNK
    sums, level = chunk_tables()
    tokens, chunks, whole = mix_specs(count, width, False)
    return pl.pallas_call(
        mix_forward_body,
        grid=(count,),
        in_specs=[
            tokens(DK), tokens(DK), tokens(width), tokens(DK), tokens(aux.shape[1]),
            chunks(1, CHUNK), whole(*sums.shape), whole(CHUNK, CHUNK),
        ],
        out_specs=[tokens(width), chunks(width, DK), chunks(CHUNK, CHUNK)],
        out_shape=[
            jax.ShapeDtypeStruct((total, width), BF),
            jax.ShapeDtypeStruct((count, width, DK), BF),
            jax.ShapeDtypeStruct((count, CHUNK, CHUNK), BF),
        ],
        scratch_shapes=[pltpu.VMEM((width, DK), F32)],
        compiler_params=pltpu.CompilerParams(
            dimension_semantics=("arbitrary",), vmem_limit_bytes=32 * 1024 * 1024
        ),
        cost_estimate=pl.CostEstimate(
            flops=total * 2 * (8 * CHUNK * DK + 2 * width * DK + CHUNK * width + 18 * CHUNK * DK),
            bytes_accessed=total * 4096, transcendentals=total * 9 * DK,
        ),
        name="mix_forward",
    )(query, key, value, log_decay, aux, seg_rows, jnp.asarray(sums, BF), jnp.asarray(level))


def mix_backward(query, key, value, log_decay, aux, seg_rows, enter, scores, grad):
    total, width = value.shape
    count = total // CHUNK
    sums, level = chunk_tables()
    tokens, chunks, whole = mix_specs(count, width, True)
    return pl.pallas_call(
        mix_backward_body,
        grid=(count,),
        in_specs=[
            tokens(DK), tokens(DK), tokens(width), tokens(DK), tokens(aux.shape[1]),
            chunks(1, CHUNK), whole(*sums.shape), whole(*sums.shape[::-1]),
            whole(CHUNK, CHUNK), whole(CHUNK, CHUNK),
            chunks(width, DK), chunks(CHUNK, CHUNK), tokens(width),
        ],
        out_specs=[tokens(DK), tokens(DK), tokens(width), tokens(DK)],
        out_shape=[
            jax.ShapeDtypeStruct((total, DK), BF),
            jax.ShapeDtypeStruct((total, DK), BF),
            jax.ShapeDtypeStruct((total, width), BF),
            jax.ShapeDtypeStruct((total, DK), F32),
        ],
        scratch_shapes=[pltpu.VMEM((width, DK), F32)],
        compiler_params=pltpu.CompilerParams(
            dimension_semantics=("arbitrary",), vmem_limit_bytes=48 * 1024 * 1024
        ),
        cost_estimate=pl.CostEstimate(
            flops=total * 2 * (14 * CHUNK * DK + 4 * width * DK + CHUNK * width + 36 * CHUNK * DK),
            bytes_accessed=total * 6144, transcendentals=total * 9 * DK,
        ),
        name="mix_backward",
    )(
        query, key, value, log_decay, aux, seg_rows, jnp.asarray(sums, BF),
        jnp.asarray(np.ascontiguousarray(sums.T), BF), jnp.asarray(level),
        jnp.asarray(np.ascontiguousarray(level.T)), enter, scores, grad,
    )


def remote(source, target, send, arrive, axis, place):
    return pltpu.make_async_remote_copy(
        src_ref=source, dst_ref=target, send_sem=send, recv_sem=arrive,
        device_id={axis: place}, device_id_type=pl.DeviceIdType.MESH,
    )


def greet(peers):
    barrier = pltpu.get_barrier_semaphore()
    number = 0
    for present, peer in peers:
        if present is True:
            pl.semaphore_signal(
                barrier, inc=1, device_id=peer, device_id_type=pl.DeviceIdType.MESH
            )
            number = number + 1
        else:

            @pl.when(present)
            def _():
                pl.semaphore_signal(
                    barrier, inc=1, device_id=peer, device_id_type=pl.DeviceIdType.MESH
                )

            number = number + jnp.where(present, 1, 0)
    pl.semaphore_wait(barrier, number)


def line_peers(axis, count):
    me = lax.axis_index(axis)
    return [(me > 0, {axis: me - 1}), (me < count - 1, {axis: me + 1})]


def all_peers(axis, count):
    me = lax.axis_index(axis)
    return [(True, {axis: lax.rem(me + away, count)}) for away in range(1, count)]


class Gather:
    def __init__(self, axis, count, x_ref, out_ref, send, arrive, local_sem):
        self.axis, self.count, self.x_ref, self.out_ref = axis, count, x_ref, out_ref
        self.send, self.arrive = send, arrive
        self.me = lax.axis_index(axis)
        self.mine = pltpu.make_async_copy(x_ref, self.block(self.me), local_sem)

    def block(self, index):
        own = self.x_ref.shape[0]
        return self.out_ref.at[pl.ds(pl.multiple_of(index * own, own), own)]

    def copy(self, direction, step, index, source):
        return remote(
            source, self.block(index), self.send.at[direction, step],
            self.arrive.at[direction, step], self.axis,
            self.me + 1 if direction == 0 else self.me - 1,
        )

    def hop(self, direction, step):
        index = self.me - step if direction == 0 else self.me + step
        return self.copy(direction, step, index, self.x_ref if step == 0 else self.block(index))

    def landed(self, direction, step):
        index = self.me - 1 - step if direction == 0 else self.me + 1 + step
        return self.copy(direction, step, index, self.block(index))

    def holds(self, direction, step):
        return self.me - step >= 0 if direction == 0 else self.me + step <= self.count - 1

    def hands_on(self, direction, step):
        inner = self.me < self.count - 1 if direction == 0 else self.me > 0
        return self.holds(direction, step) & inner

    def start(self):
        self.mine.start()
        self.run(0)

    def run(self, first, last=None):
        for step in range(first, first + 1 if last is None else last):
            for direction in (0, 1):
                if step > 0:

                    @pl.when(self.holds(direction, step))
                    def _():
                        self.landed(direction, step - 1).wait_recv()

                if step < self.count - 1:

                    @pl.when(self.hands_on(direction, step))
                    def _():
                        self.hop(direction, step).start()

    def finish(self):
        self.finish_sends()
        self.mine.wait()

    def finish_sends(self):
        for step in range(self.count - 1):
            for direction in (0, 1):

                @pl.when(self.hands_on(direction, step))
                def _():
                    self.hop(direction, step).wait_send()

    @staticmethod
    def scratch(count):
        return [
            pltpu.SemaphoreType.DMA((2, count - 1)),
            pltpu.SemaphoreType.DMA((2, count - 1)),
            pltpu.SemaphoreType.DMA,
        ]


class Swap:
    def __init__(self, axis, count, x_ref, out_ref, send, arrive, local_sem):
        self.axis, self.count, self.x_ref, self.out_ref = axis, count, x_ref, out_ref
        self.send, self.arrive = send, arrive
        self.me = lax.axis_index(axis)
        self.mine = pltpu.make_async_copy(x_ref.at[self.me], out_ref.at[self.me], local_sem)

    def hop(self, away):
        peer = lax.rem(self.me + away, self.count)
        return remote(
            self.x_ref.at[peer], self.out_ref.at[self.me], self.send.at[away - 1],
            self.arrive.at[away - 1], self.axis, peer,
        )

    def landed(self, away):
        peer = lax.rem(self.me + self.count - away, self.count)
        return remote(
            self.x_ref.at[peer], self.out_ref.at[peer], self.send.at[away - 1],
            self.arrive.at[away - 1], self.axis, peer,
        )

    def start(self):
        self.mine.start()
        for away in range(1, self.count):
            self.hop(away).start()

    def finish(self):
        for away in range(1, self.count):
            self.landed(away).wait_recv()
        for away in range(1, self.count):
            self.hop(away).wait_send()
        self.mine.wait()

    @staticmethod
    def scratch(count):
        return [
            pltpu.SemaphoreType.DMA((count - 1,)),
            pltpu.SemaphoreType.DMA((count - 1,)),
            pltpu.SemaphoreType.DMA,
        ]


class Scatter:
    def __init__(self, axis, count, pieces, x_ref, out_ref, up, down, send, arrive):
        self.axis, self.count, self.pieces = axis, count, pieces
        self.x_ref, self.out_ref, self.held_refs = x_ref, out_ref, (up, down)
        self.send, self.arrive = send, arrive
        self.me = lax.axis_index(axis)
        self.own = out_ref.shape[0]
        self.size = self.own // pieces

    def part(self, index, piece):
        start = pl.multiple_of(index * self.own + piece * self.size, self.size)
        return self.x_ref.at[pl.ds(start, self.size)]

    def held(self, direction, number, piece):
        return self.held_refs[direction].at[number, pl.ds(piece * self.size, self.size)]

    def hop(self, direction, number, piece, source=None):
        held = self.held(direction, number, piece)
        return remote(
            held if source is None else source, held, self.send.at[direction, number, piece],
            self.arrive.at[direction, number, piece], self.axis,
            self.me + 1 if direction == 0 else self.me - 1,
        )

    def target(self, direction, number):
        return self.count - 1 - number if direction == 0 else number

    def start(self, numbers=None):
        for direction in (0, 1):

            @pl.when(self.me == (0 if direction == 0 else self.count - 1))
            def _():
                for number in range(self.count - 1) if numbers is None else numbers:
                    target = self.target(direction, number)
                    for piece in range(self.pieces):
                        self.hop(direction, number, piece, self.part(target, piece)).start()

    def stage(self, direction, number, piece):
        me, target = self.me, self.target(direction, number)
        inner = me > 0 if direction == 0 else me < self.count - 1
        passed = me < target if direction == 0 else me > target
        held = self.held(direction, number, piece)

        @pl.when(inner & (passed | (me == target)))
        def _():
            self.hop(direction, number, piece).wait_recv()

        @pl.when(inner & passed)
        def _():
            mine = self.part(target, piece)[...].astype(F32)
            held[...] = (held[...].astype(F32) + mine).astype(BF)
            self.hop(direction, number, piece).start()

    def run(self, number, far):
        for order in (0, 1):

            @pl.when((self.me >= self.count // 2) == (order == 1))
            def _():
                for piece in range(self.pieces):
                    self.stage(1 - order if far else order, number, piece)

    def finish(self):
        me, count, out_ref = self.me, self.count, self.out_ref
        for piece in range(self.pieces):
            rows = pl.ds(piece * self.size, self.size)
            out_ref[rows] = self.part(me, piece)[...].astype(F32)
            for direction in (0, 1):
                for number in range(count - 1):
                    inner = me > 0 if direction == 0 else me < count - 1

                    @pl.when((me == self.target(direction, number)) & inner)
                    def _():
                        out_ref[rows] += self.held(direction, number, piece)[...].astype(F32)

        for direction in (0, 1):
            for number in range(count - 1):
                target = self.target(direction, number)

                @pl.when(me < target if direction == 0 else me > target)
                def _():
                    for piece in range(self.pieces):
                        self.hop(direction, number, piece).wait_send()

    @staticmethod
    def scratch(count, own, columns, pieces):
        return [
            pltpu.VMEM((count - 1, own, columns), BF),
            pltpu.VMEM((count - 1, own, columns), BF),
            pltpu.SemaphoreType.DMA((2, count - 1, pieces)),
            pltpu.SemaphoreType.DMA((2, count - 1, pieces)),
        ]


class CutSwap:
    def __init__(self, axis, count, refs, out_ref, send, arrive, local_sem):
        self.axis, self.count, self.refs, self.out_ref = axis, count, refs, out_ref
        self.send, self.arrive = send, arrive
        self.me = lax.axis_index(axis)
        self.widths = [ref.shape[1] // count for ref in refs]
        self.mine = [
            pltpu.make_async_copy(self.cut(i, self.me), self.slot(i, self.me), local_sem.at[i])
            for i in range(len(refs))
        ]

    def cut(self, i, index):
        size = self.widths[i]
        return self.refs[i].at[:, pl.ds(pl.multiple_of(index * size, LANES), size)]

    def slot(self, i, index):
        return self.out_ref.at[index, :, pl.ds(sum(self.widths[:i]), self.widths[i])]

    def hop(self, away, i):
        peer = lax.rem(self.me + away, self.count)
        return remote(
            self.cut(i, peer), self.slot(i, self.me), self.send.at[away - 1, i],
            self.arrive.at[away - 1, i], self.axis, peer,
        )

    def landed(self, away, i):
        peer = lax.rem(self.me + self.count - away, self.count)
        return remote(
            self.cut(i, peer), self.slot(i, peer), self.send.at[away - 1, i],
            self.arrive.at[away - 1, i], self.axis, peer,
        )

    def each(self):
        return [(away, i) for away in range(1, self.count) for i in range(len(self.refs))]

    def start(self):
        for away, i in self.each():
            self.hop(away, i).start()
        for copy in self.mine:
            copy.start()

    def finish(self):
        for away, i in self.each():
            self.landed(away, i).wait_recv()
        for away, i in self.each():
            self.hop(away, i).wait_send()
        for copy in self.mine:
            copy.wait()

    @staticmethod
    def scratch(count, parts):
        sems = pltpu.SemaphoreType.DMA((count - 1, parts))
        return [sems, sems, pltpu.SemaphoreType.DMA((parts,))]


class Deal:
    def __init__(self, axis, count, forth, x_ref, out_ref, send, arrive, local_sem):
        self.axis, self.count, self.forth = axis, count, forth
        self.x_ref, self.out_ref, self.send, self.arrive = x_ref, out_ref, send, arrive
        self.me = lax.axis_index(axis)
        self.steps = x_ref.shape[1] if forth else x_ref.shape[0]
        self.mine = [
            pltpu.make_async_copy(self.given(self.me, k), self.got(self.me, k), local_sem.at[k])
            for k in range(self.steps)
        ]

    def given(self, device, k):
        return self.x_ref.at[device, k] if self.forth else self.x_ref.at[k, device]

    def got(self, device, k):
        return self.out_ref.at[k, device] if self.forth else self.out_ref.at[device, k]

    def hop(self, away, k):
        peer = lax.rem(self.me + away, self.count)
        return remote(
            self.given(peer, k), self.got(self.me, k), self.send.at[away - 1, k],
            self.arrive.at[away - 1, k], self.axis, peer,
        )

    def landed(self, away, k):
        peer = lax.rem(self.me + self.count - away, self.count)
        return remote(
            self.given(peer, k), self.got(peer, k), self.send.at[away - 1, k],
            self.arrive.at[away - 1, k], self.axis, peer,
        )

    def each(self):
        return [(away, k) for away in range(1, self.count) for k in range(self.steps)]

    def start(self):
        for away, k in self.each():
            self.hop(away, k).start()
        for copy in self.mine:
            copy.start()

    def finish(self):
        for away, k in self.each():
            self.landed(away, k).wait_recv()
        for away, k in self.each():
            self.hop(away, k).wait_send()
        for copy in self.mine:
            copy.wait()

    @staticmethod
    def scratch(count, steps):
        sems = pltpu.SemaphoreType.DMA((count - 1, steps))
        return [sems, sems, pltpu.SemaphoreType.DMA((steps,))]


class Spread:
    def __init__(self, sizes, cuts, out_ref, far_send, far_arrive, near_send, near_arrive):
        self.X, self.C, self.Z, self.Y = sizes
        self.cuts, self.out_ref = cuts, out_ref
        self.far_send, self.far_arrive = far_send, far_arrive
        self.near_send, self.near_arrive = near_send, near_arrive
        self.x, self.c, self.z, self.y = (lax.axis_index(name) for name in OWN)
        self.others = self.X * self.Y - 1

    def across(self, offset, sign):
        down, right = offset // self.Y, offset % self.Y
        if sign < 0:
            down, right = self.X - down, self.Y - right
        return lax.rem(self.x + down, self.X), lax.rem(self.y + right, self.Y)

    def place(self, offset, c, slot):
        x, y = self.across(offset, -1)
        z = lax.rem(self.z + self.Z - slot, self.Z)
        return self.out_ref.at[((x * self.C + c) * self.Y + y) * self.Z + z]

    def far(self, offset, slot, landed=False):
        x, y = self.across(offset, 1)
        held = self.place(offset if landed else 0, self.c, slot)
        return pltpu.make_async_remote_copy(
            src_ref=held, dst_ref=held, send_sem=self.far_send.at[offset - 1, slot],
            recv_sem=self.far_arrive.at[offset - 1, slot], device_id={"x": x, "y": y},
            device_id_type=pl.DeviceIdType.MESH,
        )

    def near(self, offset, slot, landed=False):
        held = self.place(offset, 1 - self.c if landed else self.c, slot)
        return remote(
            held, held, self.near_send.at[offset, slot],
            self.near_arrive.at[offset, slot], "c", 1 - self.c,
        )

    def peers(self):
        found = all_peers("z", self.Z) + [(True, {"c": 1 - self.c})]
        for offset in range(1, self.others + 1):
            x, y = self.across(offset, 1)
            found.append((True, {"x": x, "y": y}))
        return found

    def hand_on(self, slot):
        for i in range(len(self.cuts.refs)):
            if slot > 0:
                self.cuts.landed(slot, i).wait_recv()
            else:
                self.cuts.mine[i].wait()
        for offset in range(1, self.others + 1):
            self.far(offset, slot).start()
        self.near(0, slot).start()

    def collect(self, slot):
        for offset in range(1, self.others + 1):
            self.far(offset, slot, True).wait_recv()
            self.near(offset, slot).start()

    def finish(self):
        for slot in range(self.Z):
            for offset in range(self.others + 1):
                self.near(offset, slot, True).wait_recv()
        for slot in range(self.Z):
            for offset in range(self.others + 1):
                self.near(offset, slot).wait_send()
                if offset > 0:
                    self.far(offset, slot).wait_send()
        for away, i in self.cuts.each():
            self.cuts.hop(away, i).wait_send()

    @staticmethod
    def scratch(sizes):
        X, C, Z, Y = sizes
        far = pltpu.SemaphoreType.DMA((max(X * Y - 1, 1), Z))
        near = pltpu.SemaphoreType.DMA((X * Y, Z))
        return [far, far, near, near]


class FirstCuts(CutSwap):
    def __init__(self, spread_place, count, refs, out_ref, send, arrive, local_sem):
        self.place = spread_place
        super().__init__("z", count, refs, out_ref, send, arrive, local_sem)

    def cut(self, i, index):
        return self.refs[i] if i == len(self.refs) - 1 else super().cut(i, index)

    def slot(self, i, index):
        widths = [w for w in self.widths[:-1]] + [SMALL]
        return self.out_ref.at[self.place(index), :, pl.ds(sum(widths[:i]), widths[i])]


def spread_and_gather(weights, block, other, sizes, number):
    X, C, Z, Y = sizes
    parts = len(weights)
    rows = weights[0].shape[0]
    total = sum(w.shape[1] // Z for w in weights[:-1]) + weights[-1].shape[1]

    def body(*refs):
        w_refs, x_ref, o_ref = refs[:parts], refs[parts], refs[parts + 1]
        spread_ref, out_ref, swapped_ref = refs[parts + 2 : parts + 5]
        sems = refs[parts + 5 :]
        x, c, _, y = (lax.axis_index(name) for name in OWN)
        first = FirstCuts(
            lambda index: ((x * C + c) * Y + y) * Z + index, Z, w_refs, spread_ref, *sems[:3]
        )
        spread = Spread(sizes, first, spread_ref, *sems[3:7])
        gather = Gather("z", Z, x_ref, out_ref, *sems[7:10])
        swap = CutSwap("z", Z, [o_ref], swapped_ref, *sems[10:])
        greet(spread.peers())
        first.start()
        gather.start()
        spread.hand_on(0)
        for slot in range(1, Z):
            spread.hand_on(slot)
        for step in range(1, Z):
            gather.run(step)
            if step == Z - 2:
                swap.start()
            spread.collect(step - 1)
        spread.collect(Z - 1)
        spread.finish()
        gather.finish()
        swap.finish()

    anywhere = pl.BlockSpec(memory_space=pl.ANY)
    return pl.pallas_call(
        body,
        in_specs=[anywhere] * (parts + 2),
        out_specs=[anywhere] * 3,
        out_shape=[
            jax.ShapeDtypeStruct((X * C * Y * Z, rows, total), BF),
            jax.ShapeDtypeStruct((Z * block.shape[0],) + block.shape[1:], block.dtype),
            jax.ShapeDtypeStruct((Z, rows, other.shape[1] // Z), BF),
        ],
        scratch_shapes=CutSwap.scratch(Z, parts)
        + Spread.scratch(sizes)
        + Gather.scratch(Z)
        + CutSwap.scratch(Z, 1),
        compiler_params=pltpu.CompilerParams(collective_id=number, has_side_effects=True),
        cost_estimate=pl.CostEstimate(
            flops=WAIT_FLOPS, bytes_accessed=rows * total * X * C * Y * Z * 2, transcendentals=0
        ),
        name="spread_and_gather",
    )(*weights, block, other)


def move(
    number, scatter=None, swaps=(), gathers=(), cuts=(), deals=(), extras=(), post=None
):
    in_vmem, anywhere = pl.BlockSpec(memory_space=pltpu.VMEM), pl.BlockSpec(memory_space=pl.ANY)
    values, in_specs, shapes, out_specs, scratch = [], [], [], [], []
    flags = {}

    def scale(axis):
        return lax.axis_size(axis)

    if scatter is not None:
        partial, axis = scatter
        own = partial.shape[0] // scale(axis)
        values += [partial, *extras]
        in_specs += [in_vmem] * (1 + len(extras))
        shapes.append(jax.ShapeDtypeStruct((own, partial.shape[1]), F32))
        out_specs.append(in_vmem)
        scratch += Scatter.scratch(scale(axis), own, partial.shape[1], PIECES)
        flags = dict(vmem_limit_bytes=40 * 1024 * 1024)
    for value, axis in swaps:
        values.append(value)
        in_specs.append(anywhere)
        shapes.append(jax.ShapeDtypeStruct(value.shape, value.dtype))
        out_specs.append(anywhere)
        scratch += Swap.scratch(scale(axis))
    for block, axis in gathers:
        values.append(block)
        in_specs.append(anywhere)
        shapes.append(
            jax.ShapeDtypeStruct((scale(axis) * block.shape[0], block.shape[1]), block.dtype)
        )
        out_specs.append(anywhere)
        scratch += Gather.scratch(scale(axis))

    for weights, axis in cuts:
        values += weights
        in_specs += [anywhere] * len(weights)
        wide = sum(w.shape[1] for w in weights) // scale(axis)
        shapes.append(
            jax.ShapeDtypeStruct((scale(axis), weights[0].shape[0], wide), weights[0].dtype)
        )
        out_specs.append(anywhere)
        scratch += CutSwap.scratch(scale(axis), len(weights))
    for value, axis, forth in deals:
        first, second = value.shape[:2]
        values.append(value)
        in_specs.append(anywhere)
        shapes.append(jax.ShapeDtypeStruct((second, first) + value.shape[2:], value.dtype))
        out_specs.append(anywhere)
        scratch += Deal.scratch(scale(axis), second if forth else first)

    def body(*refs):
        ins = list(refs[: len(values)])
        outs = list(refs[len(values) : len(values) + len(shapes)])
        sems = list(refs[len(values) + len(shapes) :])
        peers = {}
        adding, extra_refs, swapping, gathering = None, (), [], []
        if scatter is not None:
            axis = scatter[1]
            adding = Scatter(axis, scale(axis), PIECES, ins.pop(0), outs.pop(0), *sems[:4])
            extra_refs, ins, sems = ins[: len(extras)], ins[len(extras) :], sems[4:]
            peers[axis] = line_peers(axis, scale(axis))
        for _, axis in gathers:
            peers[axis] = line_peers(axis, scale(axis))
        for _, axis in swaps:
            peers[axis] = all_peers(axis, scale(axis))
            swapping.append(Swap(axis, scale(axis), ins.pop(0), outs.pop(0), *sems[:3]))
            sems = sems[3:]
        for _, axis in gathers:
            gathering.append(Gather(axis, scale(axis), ins.pop(0), outs.pop(0), *sems[:3]))
            sems = sems[3:]
        for weights, axis in cuts:
            peers[axis] = all_peers(axis, scale(axis))
            taken, ins = ins[: len(weights)], ins[len(weights) :]
            swapping.append(CutSwap(axis, scale(axis), taken, outs.pop(0), *sems[:3]))
            sems = sems[3:]
        for _, axis, forth in deals:
            peers[axis] = all_peers(axis, scale(axis))
            swapping.append(
                Deal(axis, scale(axis), forth, ins.pop(0), outs.pop(0), *sems[:3])
            )
            sems = sems[3:]
        greet([peer for found in peers.values() for peer in found])
        for part in gathering + ([adding] if adding else []) + swapping:
            part.start()
        steps = max([part.count for part in gathering + ([adding] if adding else [])] + [0])
        for part in gathering:
            part.run(1)
        for step in range(1, steps):
            if adding:
                adding.run(step - 1, False)
            for part in gathering:
                if step + 1 < part.count:
                    part.run(step + 1)
            if adding:
                adding.run(step - 1, True)
        if adding:
            adding.finish()
            if post is not None:
                adding.out_ref[...] = post(adding.out_ref[...], *[r[...] for r in extra_refs])
        for part in swapping + gathering:
            part.finish()

    size = sum(v.size for v in values)
    return pl.pallas_call(
        body,
        in_specs=in_specs,
        out_specs=out_specs,
        out_shape=shapes,
        scratch_shapes=scratch,
        compiler_params=pltpu.CompilerParams(
            collective_id=number, has_side_effects=True, **flags
        ),
        cost_estimate=pl.CostEstimate(
            flops=WAIT_FLOPS, bytes_accessed=size * 4, transcendentals=0
        ),
        name="move",
    )(*values)


def feed_forward(normed_own, mlp_piece, cotangent, number):
    count = lax.axis_size("z")
    own, width = normed_own.shape
    group, ff = own * count, mlp_piece.shape[1] // 3
    half = group // 2
    block = width // (2 * lax.axis_size("x"))

    def body(x_ref, w_hbm, c_hbm, sum_ref, down_ref, grad_hbm,
             w_ref, d_ref, c_ref, normed, hidden_grad, hidden, grads, partial, stage, received,
             load_sem, store_sem, pair_send, pair_arrive, gather_send, gather_arrive, local_sem, up, down, send, arrive):
        me, core = lax.axis_index("z"), lax.axis_index("c")
        loads = [
            pltpu.make_async_copy(source, target, load_sem.at[i])
            for i, (source, target) in enumerate(
                [
                    (c_hbm, c_ref),
                    (w_hbm.at[:, pl.ds(2 * ff, ff)], d_ref),
                    (w_hbm.at[:, pl.ds(0, 2 * ff)], w_ref),
                ]
            )
        ]
        for load in loads:
            load.start()
        gather = Gather("z", count, x_ref, normed, gather_send, gather_arrive, local_sem)
        scatter = Scatter("z", count, PIECES, partial, sum_ref, up, down, send, arrive)
        greet(line_peers("z", count) + [(True, {"c": 1 - core})])
        gather.start()
        loads[0].wait()
        loads[1].wait()

        def tile_of(index, size):
            return pl.ds(pl.multiple_of(index * size, size), size)

        def spans(total):
            return [pl.ds(at, min(TILE, total - at)) for at in range(0, total, TILE)]

        for at in spans(ff):
            hidden_grad[:, at] = dot_plain(c_ref[...], d_ref[:, at])
        loads[2].wait()
        lower = me < count // 2
        nearer = me // (count // 2)

        def forward(rows):
            for at in spans(ff):
                up_at = pl.ds(ff + at.start, at.size)
                gate = dot_plain(normed[rows], w_ref[:, at])
                upper = dot_plain(normed[rows], w_ref[:, up_at])
                grad = hidden_grad[rows, at]
                sig = jax.nn.sigmoid(gate)
                silu = gate * sig
                hidden[rows, at] = (silu * upper).astype(BF)
                grad_gate = grad * upper * sig * (1.0 + gate * (1.0 - sig))
                grads[rows, at] = grad_gate.astype(BF)
                grads[rows, up_at] = (grad * silu).astype(BF)

        def backward(rows):
            for at in spans(width):
                partial[rows, at] = dot_rows(grads[rows], w_ref[at]).astype(BF)

        kept = width // 2 // TILE
        rows_kept = functools.partial(rows_of_core, block)

        def store(number):
            return pltpu.make_async_copy(
                stage.at[number % 2], grad_hbm.at[pl.ds(number * TILE, TILE)],
                store_sem.at[number % 2],
            )

        def pass_over(number):
            return remote(
                stage.at[number % 2], received.at[number], pair_send.at[number % 2],
                pair_arrive.at[number], "c", 1 - core,
            )

        def weight_rows(i):
            ours, number = i >= kept, i % kept
            if i >= 2:
                if i - 2 >= kept:
                    store(i - 2 - kept).wait()
                else:
                    pass_over(i - 2).wait_send()
            at = rows_kept(number, core if ours else 1 - core)
            slot = i % 2
            top = dot_cols(normed[:, at], grads[...])
            low = dot_cols(c_ref[:, at], hidden[...])
            if ours:
                pass_over(number).wait_recv()
                top = top + received[number, :, : 2 * ff].astype(F32)
                low = low + received[number, :, 2 * ff :].astype(F32)
            stage[slot, :, : 2 * ff] = top.astype(BF)
            stage[slot, :, 2 * ff :] = low.astype(BF)
            if ours:
                store(number).start()
            else:
                pass_over(number).start()
            at = pl.ds(i * TILE, TILE)
            down_ref[:, at] = dot_rows(hidden[...], d_ref[at]).astype(BF)

        def away(near):
            block = jnp.where(lower, count // 2, count // 2 - 1)
            end = jnp.where(lower, count - 1, 0)
            return tile_of(block if near else end, own)

        gather.run(1)
        gather.mine.wait()
        forward(tile_of(nearer, half))
        gather.run(2)
        forward(away(True))
        gather.run(3)
        forward(away(False))
        backward(away(False))
        scatter.start([0])
        backward(away(True))
        scatter.start([1])
        backward(tile_of(nearer, half))
        scatter.start([2])
        units = list(range(width // TILE))
        stages = [(step, far) for step in range(count - 1) for far in (False, True)]
        spare = len(units) - len(stages)
        for i in units[: max(spare, 0)]:
            weight_rows(i)
        rest = units[max(spare, 0) :]
        for step, far in stages:
            scatter.run(step, far)
            if rest:
                weight_rows(rest.pop(0))
        scatter.finish()
        gather.finish_sends()
        for number in range(kept - 2, kept):
            store(number).wait()

    in_vmem, anywhere = pl.BlockSpec(memory_space=pltpu.VMEM), pl.BlockSpec(memory_space=pl.ANY)
    return pl.pallas_call(
        body,
        in_specs=[in_vmem, anywhere, anywhere],
        out_specs=[in_vmem, in_vmem, anywhere],
        out_shape=[
            jax.ShapeDtypeStruct((own, width), F32),
            jax.ShapeDtypeStruct((group, width), BF),
            jax.ShapeDtypeStruct((width // 2, 3 * ff), BF),
        ],
        scratch_shapes=[
            pltpu.VMEM((width, 2 * ff), BF),
            pltpu.VMEM((width, ff), BF),
            pltpu.VMEM((group, width), BF),
            pltpu.VMEM((group, width), BF),
            pltpu.VMEM((group, ff), F32),
            pltpu.VMEM((group, ff), BF),
            pltpu.VMEM((group, 2 * ff), BF),
            pltpu.VMEM((group, width), BF),
            pltpu.VMEM((2, TILE, 3 * ff), BF),
            pltpu.VMEM((width // 2 // TILE, TILE, 3 * ff), BF),
            pltpu.SemaphoreType.DMA((3,)),
            pltpu.SemaphoreType.DMA((2,)),
            pltpu.SemaphoreType.DMA((2,)),
            pltpu.SemaphoreType.DMA((width // 2 // TILE,)),
        ]
        + Gather.scratch(count)
        + Scatter.scratch(count, own, width, PIECES),
        compiler_params=pltpu.CompilerParams(
            collective_id=number, has_side_effects=True, vmem_limit_bytes=60 * 1024 * 1024
        ),
        cost_estimate=pl.CostEstimate(
            flops=WAIT_FLOPS, bytes_accessed=width * ff * 12, transcendentals=0
        ),
        name="feed_forward",
    )(normed_own, mlp_piece, cotangent)


def rows_of_core(block, number, by):
    per = block // TILE
    start = (number // per * 2 + by) * block + number % per * TILE
    return pl.ds(pl.multiple_of(start, TILE), TILE)


def attention_end(
    grad_heads, normed, small, weights, side, extras, post, sizes, number
):
    X, C, Z, Y = sizes
    group, total = grad_heads.shape
    width = normed.shape[1]
    own = group // Z
    near, skip = 2 * DK + DV, 2 * DK + 2 * DV
    wide = near + SMALL
    rows = width // (X * C * Y * Z)
    piece = Z * rows
    block = width // (C * X)
    kept = width // 2 // TILE
    others = X * Y - 1

    def body(*refs):
        gh_ref, normed_ref, small_ref = refs[:3]
        extra_refs = refs[3 : 3 + len(extras)]
        w_hbm, side_ref, out_ref, near_out, side_out = refs[3 + len(extras) : 8 + len(extras)]
        (w_ref, partial, given, received, sums, parts, final, load_sem, pair_send, pair_arrive,
         far_send, far_arrive) = refs[8 + len(extras) : 20 + len(extras)]
        sems = refs[20 + len(extras) :]
        x, core, me, y = (lax.axis_index(name) for name in OWN)
        scatter = Scatter("z", Z, PIECES, partial, out_ref, *sems[:4])
        near_swap = Swap("z", Z, final, near_out, *sems[4:7])
        side_swap = Swap("z", Z, side_ref, side_out, *sems[7:10])
        load = pltpu.make_async_copy(w_hbm, w_ref, load_sem)
        load.start()

        def across(offset, sign):
            down, right = offset // Y, offset % Y
            if sign < 0:
                down, right = X - down, Y - right
            return lax.rem(x + down, X), lax.rem(y + right, Y)

        peers = all_peers("z", Z) + [(True, {"c": 1 - core})]
        for offset in range(1, others + 1):
            to_x, to_y = across(offset, 1)
            peers.append((True, {"x": to_x, "y": to_y}))
        greet(peers)

        def backward(at_rows):
            for at in range(0, width, TILE):
                columns = pl.ds(at, TILE)
                partial[at_rows, columns] = dot_rows(gh_ref[at_rows], w_ref[columns]).astype(BF)

        def rows_at(index, size):
            return pl.ds(pl.multiple_of(index * size, size), size)

        lower = me < Z // 2
        load.wait()
        backward(rows_at(jnp.where(lower, Z - 1, 0), own))
        scatter.start([0])
        backward(rows_at(jnp.where(lower, Z // 2, Z // 2 - 1), own))
        scatter.start([1])
        backward(rows_at(me // (Z // 2), group // 2))
        scatter.start([2])

        def pass_over(i):
            return remote(
                given.at[i], received.at[i], pair_send.at[i], pair_arrive.at[i], "c", 1 - core
            )

        def products(i, by):
            at = rows_of_core(block, i, by)
            top = dot_cols(normed_ref[:, at], gh_ref[:, :near])
            low = dot_cols(normed_ref[:, at], gh_ref[:, skip:]) + small_ref[at]
            return top, low

        for i in range(kept):
            top, low = products(i, 1 - core)
            given[i, :, :near] = top.astype(BF)
            given[i, :, near:] = low.astype(BF)
            pass_over(i).start()
        for i in range(kept):
            top, low = products(i, core)
            pass_over(i).wait_recv()
            at = pl.ds(i * TILE, TILE)
            sums[at, :near] = (top + received[i, :, :near].astype(F32)).astype(BF)
            sums[at, near:] = (low + received[i, :, near:].astype(F32)).astype(BF)

        def far(offset, by=1):
            to_x, to_y = across(offset, by)
            return pltpu.make_async_remote_copy(
                src_ref=sums.at[rows_at(to_x * Y + to_y, piece)], dst_ref=parts.at[offset - 1],
                send_sem=far_send.at[offset - 1], recv_sem=far_arrive.at[offset - 1],
                device_id={"x": to_x, "y": to_y}, device_id_type=pl.DeviceIdType.MESH,
            )

        for offset in range(1, others + 1):
            far(offset).start()
        for step in range(Z - 2):
            scatter.run(step, False)
            scatter.run(step, True)
        side_swap.start()
        own_sum = sums[rows_at(x * Y + y, piece)].astype(F32)
        for offset in range(1, others + 1):
            far(offset).wait_recv()
            own_sum = own_sum + parts[offset - 1].astype(F32)
        for index in range(Z):
            final[index] = own_sum[index * rows : (index + 1) * rows].astype(BF)
        near_swap.start()
        scatter.run(Z - 2, False)
        scatter.run(Z - 2, True)
        scatter.finish()
        out_ref[...] = post(out_ref[...], *[r[...] for r in extra_refs])
        side_swap.finish()
        near_swap.finish()
        for offset in range(1, others + 1):
            far(offset).wait_send()
        for i in range(kept):
            pass_over(i).wait_send()

    in_vmem, anywhere = pl.BlockSpec(memory_space=pltpu.VMEM), pl.BlockSpec(memory_space=pl.ANY)
    return pl.pallas_call(
        body,
        in_specs=[in_vmem] * (3 + len(extras)) + [anywhere] * 2,
        out_specs=[in_vmem, anywhere, anywhere],
        out_shape=[
            jax.ShapeDtypeStruct((own, width), F32),
            jax.ShapeDtypeStruct((Z, rows, wide), BF),
            jax.ShapeDtypeStruct(side.shape, BF),
        ],
        scratch_shapes=[
            pltpu.VMEM((width, total), BF),
            pltpu.VMEM((group, width), BF),
            pltpu.VMEM((kept, TILE, wide), BF),
            pltpu.VMEM((kept, TILE, wide), BF),
            pltpu.VMEM((width // 2, wide), BF),
            pltpu.VMEM((max(others, 1), piece, wide), BF),
            pltpu.VMEM((Z, rows, wide), BF),
            pltpu.SemaphoreType.DMA,
            pltpu.SemaphoreType.DMA((kept,)),
            pltpu.SemaphoreType.DMA((kept,)),
            pltpu.SemaphoreType.DMA((max(others, 1),)),
            pltpu.SemaphoreType.DMA((max(others, 1),)),
        ]
        + Scatter.scratch(Z, own, width, PIECES)
        + Swap.scratch(Z)
        + Swap.scratch(Z),
        compiler_params=pltpu.CompilerParams(
            collective_id=number, has_side_effects=True, vmem_limit_bytes=56 * 1024 * 1024
        ),
        cost_estimate=pl.CostEstimate(
            flops=WAIT_FLOPS, bytes_accessed=width * total * 6, transcendentals=0
        ),
        name="attention_end",
    )(grad_heads, normed, small, *extras, weights, side)


def join(values, parts, weights=()):
    Z, rows = values[0].shape[:2]

    def body(*refs):
        ins, refs = refs[: len(values)], refs[len(values) :]
        w_refs, outs = refs[: len(weights)], refs[len(weights) :]
        moment = jnp.zeros((rows, 1), F32)
        for number, (out_ref, (index, start, size)) in enumerate(zip(outs, parts)):
            held = ins[index][0, :, start : start + size].astype(F32)
            out_ref[...] = held
            if number < len(weights):
                product = held * w_refs[number][...].astype(F32)
                moment = moment + jnp.sum(product, axis=1, keepdims=True)
        if weights:
            before = jnp.where(pl.program_id(0) == 0, 0.0, outs[-1][...])
            outs[-1][...] = before + moment

    return pl.pallas_call(
        body,
        grid=(Z,),
        in_specs=[pl.BlockSpec((1,) + v.shape[1:], lambda i: (i, 0, 0)) for v in values]
        + [pl.BlockSpec((rows, w.shape[1] // Z), lambda i: (0, i)) for w in weights],
        out_specs=[pl.BlockSpec((rows, part[2]), lambda i: (0, i)) for part in parts]
        + [pl.BlockSpec((rows, LANES), lambda i: (0, 0))] * (len(weights) > 0),
        out_shape=[jax.ShapeDtypeStruct((rows, Z * part[2]), F32) for part in parts]
        + [jax.ShapeDtypeStruct((rows, LANES), F32)] * (len(weights) > 0),
        compiler_params=pltpu.CompilerParams(dimension_semantics=("arbitrary",)),
        name="join",
    )(*values, *weights)


def local(
    tokens, doc_lengths, cotangent, attn_gain, query_weight, key_weight, value_weight, gate_weight,
    rank_in, rank_out, decay_bias, head_gain, out_weight, mlp_gain, mlp_gate_weight,
    mlp_up_weight, down_weight,
):
    own, width = tokens.shape
    rows = query_weight.shape[0]
    X, C, Z, Y = (lax.axis_size(name) for name in OWN)
    z = lax.axis_index("z")
    group = own * Z
    total = group * Y
    ff = down_weight.shape[1] // Z
    dvp = DV // Y

    def blocked(value):
        lead = value.shape[:-1]
        cut = value.reshape(lead + (X, C, Z, Y, rows))
        return jnp.swapaxes(cut, -3, -2).reshape(lead + (width,))

    def straight(value):
        found = []
        for start in range(0, width, Z * Y * rows):
            for at_z in range(Z):
                for at_y in range(Y):
                    first_lane = start + (at_y * Z + at_z) * rows
                    found.append(value[:, first_lane : first_lane + rows])
        return jnp.concatenate(found, axis=1)

    def pad_rows(value):
        flat = value.reshape(value.shape[0], -1)
        return jnp.pad(flat, ((0, rows - flat.shape[0]), (0, 0)))

    numbers = iter(range(32))

    def deal(value, forth):
        return move(next(numbers), deals=[(value, "y", forth)])[0]

    def after(value, *others):
        return lax.optimization_barrier((value,) + others)[0]

    def scatter_rest(value, axes=REST):
        sums = lax.psum_scatter(value, axes, scatter_dimension=0, tiled=True)
        return sums.reshape(Z, rows, -1)

    def gather_rest(value, axes=REST):
        return lax.all_gather(value.reshape(Z * rows, -1), axes, axis=0, tiled=True)

    small = jnp.concatenate(
        [
            rank_in, pad_rows(attn_gain), pad_rows(mlp_gain), pad_rows(rank_out),
            pad_rows(decay_bias), pad_rows(head_gain),
        ],
        axis=1,
    )
    small = jnp.pad(small, ((0, 0), (0, SMALL - small.shape[1])))
    own_tokens = blocked(tokens)
    input_weights, group_tokens, out_weights = spread_and_gather(
        [query_weight, key_weight, value_weight, gate_weight, small],
        own_tokens, out_weight, (X, C, Z, Y), next(numbers),
    )
    input_weights = input_weights.reshape(width, -1)

    projected = 2 * DK + 2 * DV
    near = 2 * DK + DV
    small_all = input_weights[:, projected:].astype(F32)

    def device_rows(value, count):
        cut = value.reshape(X, C, Y, Z, rows, -1)[:, :, :, :, : rows // count]
        return jnp.swapaxes(cut, 2, 3).reshape(width // count, -1)

    attn_gain_all = small_all[:, R]
    mlp_gain_all = small_all[:, R + 1]
    rank_out_all = device_rows(small_all[:, R + 2 : 2 * R + 2], width // (H * DK))
    bias_all = device_rows(small_all[:, 2 * R + 2 : 2 * R + 3], width // (H * DK))
    head_gain_all = device_rows(small_all[:, 2 * R + 3 : 2 * R + 4], width // DV)[:, 0]
    rank_out_z = lax.dynamic_slice_in_dim(rank_out_all, z * DK, DK).astype(BF)
    bias_z = lax.dynamic_slice_in_dim(bias_all, z * DK, DK)[:, 0]

    def to_device_rows(value, count):
        cut = value.reshape(X, C, Z, Y, rows // count, -1)
        cut = jnp.swapaxes(cut, 2, 3)
        cut = jnp.pad(cut, ((0, 0),) * 4 + ((0, rows - rows // count), (0, 0)))
        return cut.reshape(width, -1)

    def at_head(value):
        return lax.dynamic_update_slice_in_dim(
            jnp.zeros((H * DK, value.shape[1]), F32), value, z * DK, 0
        )

    rows_in = group_tokens.astype(F32)
    scale_in = lax.rsqrt(jnp.mean(rows_in * rows_in, axis=1, keepdims=True) + norm_eps)
    normed_in = (rows_in * scale_in * attn_gain_all).astype(BF)
    heads = dot_plain(normed_in, input_weights)
    out_gate = heads[:, 2 * DK + DV : projected]
    low = heads.astype(BF)
    rank_beside_one = jnp.concatenate(
        [
            jnp.zeros((group, RANK_AT), BF), low[:, projected : projected + R],
            jnp.ones((group, 1), BF), jnp.zeros((group, SMALL - RANK_AT - R - 1), BF),
        ],
        axis=1,
    )
    shared = jnp.concatenate([low[:, : 2 * DK], low[:, projected:]], axis=1)
    values = jnp.swapaxes(low[:, 2 * DK : 2 * DK + DV].reshape(group, Y, dvp), 0, 1)
    sent = jnp.concatenate([jnp.broadcast_to(shared[None], (Y,) + shared.shape), values], axis=2)
    mlp_weights, sequence = move(
        next(numbers), cuts=[([mlp_gate_weight, mlp_up_weight, down_weight], "z")],
        deals=[(sent.reshape(Y, Z, own, -1), "y", True)],
    )
    out_piece = gather_rest(out_weights)
    mlp_piece = gather_rest(mlp_weights)
    sequence = sequence.reshape(total, -1)
    queries = sequence[:, :DK]
    keys = sequence[:, DK : 2 * DK]
    rank_low = sequence[:, 2 * DK : 2 * DK + R]
    value_part = sequence[:, 2 * DK + SMALL :]
    decay_logit = dot_rows(rank_low, rank_out_z) + bias_z
    log_decay = jax.nn.log_sigmoid(decay_logit) / decay_norm

    doc_ends = jnp.cumsum(doc_lengths[0])
    positions = lax.iota(jnp.int32, total)
    segments = jnp.sum((doc_ends[None, :] <= positions[:, None]).astype(jnp.int32), axis=1)
    cut = segments.reshape(-1, CHUNK)
    last = cut[:, CHUNK - 1 :]
    before = jnp.concatenate([jnp.full((1, 1), -1, jnp.int32), last[:-1]], axis=0)
    aux = jnp.stack(
        [cut == before, cut == last, cut, jnp.broadcast_to(last == before, cut.shape)], axis=-1
    )
    aux = aux.reshape(total, 4).astype(F32)
    seg_rows = cut.astype(F32)[:, None, :]

    mixed_part, enter, scores = mix_forward(queries, keys, value_part, log_decay, aux, seg_rows)
    mixed_part = deal(mixed_part.reshape(Z, Y, own, dvp), False).reshape(Y, group, dvp)
    mixed = jnp.swapaxes(mixed_part, 0, 1).reshape(group, DV).astype(F32)

    head_scale = lax.rsqrt(jnp.mean(mixed * mixed, axis=1, keepdims=True) + head_eps)
    head_hat = mixed * head_scale
    head_out = head_hat * head_gain_all
    sig_out = jax.nn.sigmoid(out_gate)
    silu_out = out_gate * sig_out
    gated = (head_out * silu_out).astype(BF)
    own_cotangent = blocked(cotangent)
    residual, group_cotangent = move(
        next(numbers), scatter=(dot_rows(gated, out_piece).astype(BF), "z"),
        gathers=[(own_cotangent, "z")], extras=[own_tokens],
        post=lambda total_sum, x: total_sum + x.astype(F32),
    )
    scale_mid = lax.rsqrt(jnp.mean(residual * residual, axis=1, keepdims=True) + norm_eps)
    hat_mid = residual * scale_mid
    normed_mlp = (hat_mid * mlp_gain_all).astype(BF)
    grad_normed_mlp, out_partial, mlp_partial = feed_forward(
        normed_mlp, mlp_piece, group_cotangent, next(numbers)
    )
    mlp_sums = scatter_rest(mlp_partial, ("x", "y"))

    scaled = grad_normed_mlp * mlp_gain_all
    grad_residual = own_cotangent.astype(F32) + scale_mid * (
        scaled - hat_mid * jnp.mean(scaled * hat_mid, axis=1, keepdims=True)
    )
    branch_own = grad_residual.astype(BF)
    layer_out, grad_branch = move(
        next(numbers), scatter=(out_partial, "z"), gathers=[(branch_own, "z")],
        extras=[residual], post=lambda total_sum, rest: straight(total_sum + rest),
    )
    grad_gated = dot_plain(grad_branch, out_piece)
    grad_head = grad_gated * silu_out
    head_gain_part = jnp.sum(grad_head * head_hat, axis=0)
    head_small = jnp.pad(
        to_device_rows(head_gain_part[:, None], width // DV), ((0, 0), (HEAD_AT, SMALL - HEAD_AT - 1))
    )
    from_head = grad_head * head_gain_all
    grad_mixed = head_scale * (
        from_head - head_hat * jnp.mean(from_head * head_hat, axis=1, keepdims=True)
    )
    grad_out_gate = (grad_gated * head_out * sig_out * (1.0 + out_gate * (1.0 - sig_out))).astype(BF)
    grad_cut = jnp.swapaxes(grad_mixed.astype(BF).reshape(group, Y, dvp), 0, 1)
    grad_part = deal(grad_cut.reshape(Y, Z, own, dvp), True).reshape(total, dvp)
    dq, dk, dv, dld = mix_backward(
        queries, keys, value_part, log_decay, aux, seg_rows, enter, scores, grad_part
    )
    dlogit = (dld * jax.nn.sigmoid(-decay_logit) / decay_norm).astype(BF)
    back = jnp.concatenate([dq, dk, dlogit, dv], axis=1).reshape(Z, Y, own, -1)
    side_partial = jnp.concatenate(
        [dot_cols(normed_in, grad_out_gate), dot_cols(grad_branch, gated)], axis=1
    ).astype(BF)
    back, side_partial = lax.optimization_barrier((back, side_partial))
    side_sums = scatter_rest(after(side_partial, mlp_sums))
    mlp_rows, back = move(
        next(numbers), swaps=[(mlp_sums, "z")], deals=[(back, "y", False)]
    )
    back = back.reshape(Y, group, -1)
    summed = jnp.sum(back[:, :, : 3 * DK].astype(F32), axis=0).astype(BF)
    grad_value = jnp.swapaxes(back[:, :, 3 * DK :], 0, 1).reshape(group, DV)
    grad_logit = summed[:, 2 * DK :]
    rank_out_part = dot_cols(grad_logit, rank_beside_one)
    grad_rank = dot_plain(grad_logit, rank_out_z).astype(BF)
    grad_heads = jnp.concatenate(
        [
            summed[:, : 2 * DK], grad_value, grad_out_gate,
            jnp.pad(grad_rank, ((0, 0), (0, SMALL - R))),
        ],
        axis=1,
    )
    small_part = to_device_rows(at_head(rank_out_part), width // (H * DK)) + head_small

    def finish_tokens(back_sum, x, grad_res, gain):
        held = x.astype(F32)
        scale = lax.rsqrt(jnp.mean(held * held, axis=1, keepdims=True) + norm_eps)
        hat = held * scale
        scaled = back_sum * gain
        mean = jnp.mean(scaled * hat, axis=1, keepdims=True)
        return straight(grad_res + scale * (scaled - hat * mean))

    tokens_grad, near_rows, side_rows = attention_end(
        grad_heads, normed_in, small_part, input_weights, side_sums,
        [own_tokens, grad_residual, attn_gain_all[None]], finish_tokens, (X, C, Z, Y),
        next(numbers),
    )
    *mlp_grads, mlp_moments = join(
        [mlp_rows], [(0, 0, ff), (0, ff, ff), (0, 2 * ff, ff)], [mlp_gate_weight, mlp_up_weight]
    )
    query_grad, key_grad, value_grad, gate_grad, out_grad, moments = join(
        [near_rows, side_rows],
        [
            (0, 0, DK), (0, DK, DK), (0, 2 * DK, DV), (1, 0, DV), (1, DV, DV),
        ],
        [query_weight, key_weight, value_weight, gate_weight],
    )
    small_rows = jnp.sum(near_rows[:, :, near : near + SMALL].astype(F32), axis=0)
    rank_in_grad = small_rows[:, :R]
    moment = moments[:, 0] + jnp.sum(rank_in_grad * rank_in.astype(F32), axis=1)
    return (
        layer_out,
        tokens_grad,
        moment / attn_gain.astype(F32),
        query_grad,
        key_grad,
        value_grad,
        gate_grad,
        rank_in_grad,
        small_rows[: rows * H * DK // width, RANK_AT : RANK_AT + R],
        small_rows[: rows * H * DK // width, RANK_AT + R],
        small_rows[: rows * DV // width, HEAD_AT],
        out_grad,
        mlp_moments[:, 0] / mlp_gain.astype(F32),
        *mlp_grads,
    )


def solution(mesh):
    groups, places = mesh.shape["grp"], mesh.shape["seq"]
    wide = Mesh(mesh.devices.reshape(groups // 2, 2, H, places // H), OWN)
    split = P(OWN, None)
    line = P(OWN)
    by_sequence = P(("x", "c"), None)
    placed = (
        split, by_sequence, split, line, split, split, split, split, split, split,
        line, line, split, line, split, split, split,
    )
    return jax.shard_map(
        local,
        mesh=wide,
        in_specs=placed,
        out_specs=(
            split, split, line, split, split, split, split, split, split, line, line, split,
            line, split, split, split,
        ),
        check_vma=False,
    )
```

profile of v0, /device:TPU:9, one launch (start us, length us, event | category | flops | bytes accessed | tf_op | source)
XLA Modules:
  0.0 586.4 jit_solution(16381590125765590534)
XLA Ops:
  14.9 60.7 %spread_and_gather.1 = (bf16[32,64,1664]{2,1,0:T(8,128)(2,1)}, bf16[512,2048]{1,0:T(8,128)(2,1)}, bf16[4,64,512]{2,1,0:T(8,128)(2,1)}) custom-call(bf16[64,1024]{1,0:T(8,128)(2,1)} %refs_2_.6, bf16[64,1024]{1,0:T(8,128)(2,1)} %refs_3_.3, bf16[64,2048]{1,0:T(8,128)(2,1)} %refs_4_.1, bf16[64,2048]{1,0:T(8,128)(2,1)} %refs_5_.1, bf16[64,128]{1,0:T(8,128)(2,1)} %pad.35.refs_4_, ...), custom_call_target="tpu_custom_call" | custom-call | flops 100000000 | bytes 6815744 | tf_op jit(solution)/shard_map/spread_and_gather/pallas_call | solution.py:746
  76.9 2.2 slice_reduce_fusion.1
  80.4 5.7 fusion.26
  88.8 55.1 %move.6 = (bf16[4,64,4224]{2,1,0:T(8,128)(2,1)}, bf16[4,2,128,896]{3,2,1,0:T(8,128)(2,1)}) custom-call(bf16[64,5632]{1,0:T(8,128)(2,1)} %refs_1_.5, bf16[64,5632]{1,0:T(8,128)(2,1)} %refs_2_.7, bf16[64,5632]{1,0:T(8,128)(2,1)} %refs_2_.5, bf16[2,4,128,896]{3,2,1,0:T(8,128)(2,1)} %bitcast.95), custom_call_target="tpu_custom_call" | custom-call | flops 100000000 | bytes 7995392 | tf_op jit(solution)/shard_map/move/pallas_call | solution.py:871
  148.6 3.0 fusion.6
  151.7 7.8 %mix_forward.1 = (bf16[1024,256]{1,0:T(8,128)(2,1)S(1)}, bf16[8,256,256]{2,1,0:T(8,128)(2,1)S(1)}, bf16[8,128,128]{2,1,0:T(8,128)(2,1)S(1)}) custom-call(bf16[1024,256]{1,0:T(8,128)(2,1)S(1)} %get-tuple-element.169.q_ref, bf16[1024,256]{1,0:T(8,128)(2,1)S(1)} %get-tuple-element.168.k_ref, bf16[1024,256]{1,0:T(8,128)(2,1)S(1)} %get-tuple-element.167.v_ref, ...), custom_call_target="tpu_custom_call" | custom-call | flops 2080374784 | bytes 4194304 | tf_op jit(solution)/shard_map/mix_forward/pallas_call | solution.py:204
  162.0 13.9 %move.7 = bf16[2,4,128,256]{3,2,1,0:T(8,128)(2,1)} custom-call(bf16[4,2,128,256]{3,2,1,0:T(8,128)(2,1)} %bitcast.85), custom_call_target="tpu_custom_call" | custom-call | flops 100000000 | bytes 1048576 | tf_op jit(solution)/shard_map/move/pallas_call | solution.py:871
  181.0 2.9 convolution_convert_fusion.2.refs_0_
  184.0 46.4 %move.8 = (f32[128,2048]{1,0:T(8,128)S(1)}, bf16[512,2048]{1,0:T(8,128)(2,1)S(1)}) custom-call(bf16[512,2048]{1,0:T(8,128)(2,1)S(1)} %convolution_convert_fusion.2.refs_0_, bf16[128,2048]{1,0:T(8,128)(2,1)S(1)} %copy-done, bf16[128,2048]{1,0:T(8,128)(2,1)S(1)} %copy.253.refs_2_), custom_call_target="tpu_custom_call" | custom-call | flops 100000000 | bytes 6291456 | tf_op jit(solution)/shard_map/move/pallas_call | solution.py:871
  232.8 9.5 %all-gather.5.cloned.1.call-done.w_hbm = bf16[2048,4224]{1,0:T(8,128)(2,1)} async-done(((bf16[256,4224]{1,0:T(8,128)(2,1)}), bf16[2048,4224]{1,0:T(8,128)(2,1)}) %all-gather.5.cloned.1.call-update) | async-done | bytes 17301520 | tf_op jit(solution)/shard_map/all_gather | solution.py:1288
  242.3 84.7 %feed_forward.1 = (f32[128,2048]{1,0:T(8,128)}, bf16[512,2048]{1,0:T(8,128)(2,1)}, bf16[1024,4224]{1,0:T(8,128)(2,1)}) custom-call(bf16[128,2048]{1,0:T(8,128)(2,1)} %multiply_convert_fusion.3.x_ref, bf16[2048,4224]{1,0:T(8,128)(2,1)} %all-gather.5.cloned.1.call-done.w_hbm, bf16[512,2048]{1,0:T(8,128)(2,1)} %copy-done.1), custom_call_target="tpu_custom_call" | custom-call | flops 100000000 | bytes 34603008 | tf_op jit(solution)/shard_map/feed_forward/pallas_call | solution.py:1019
  330.8 44.6 %move.9 = (f32[128,2048]{1,0:T(8,128)S(1)}, bf16[512,2048]{1,0:T(8,128)(2,1)S(1)}) custom-call(bf16[512,2048]{1,0:T(8,128)(2,1)S(1)} %copy-done.2, f32[128,2048]{1,0:T(8,128)S(1)} %get-tuple-element.58.refs_1_, bf16[128,2048]{1,0:T(8,128)(2,1)S(1)} %get-tuple-element.163.refs_2_), custom_call_target="tpu_custom_call" | custom-call | flops 100000000 | bytes 6291456 | tf_op jit(solution)/shard_map/move/pallas_call | solution.py:871
  375.5 2.1 multiply_reduce_fusion
  379.2 2.1 reshape.290
  381.3 1.9 copy.256
  383.2 9.6 %move.10 = bf16[4,2,128,256]{3,2,1,0:T(8,128)(2,1)} custom-call(bf16[2,4,128,256]{3,2,1,0:T(8,128)(2,1)} %bitcast.108), custom_call_target="tpu_custom_call" | custom-call | flops 100000000 | bytes 1048576 | tf_op jit(solution)/shard_map/move/pallas_call | solution.py:871
  396.7 13.6 %mix_backward.1 = (bf16[1024,256]{1,0:T(8,128)(2,1)S(1)}, bf16[1024,256]{1,0:T(8,128)(2,1)S(1)}, bf16[1024,256]{1,0:T(8,128)(2,1)S(1)}, f32[1024,256]{1,0:T(8,128)}) custom-call(bf16[1024,256]{1,0:T(8,128)(2,1)S(1)} %copy-done.8, bf16[1024,256]{1,0:T(8,128)(2,1)S(1)} %copy-done.6, bf16[1024,256]{1,0:T(8,128)(2,1)S(1)} %get-tuple-element.167.v_ref, ...), custom_call_target="tpu_custom_call" | custom-call | flops 3959422976 | bytes 6291456 | tf_op jit(solution)/shard_map/mix_backward/pallas_call | solution.py:234
  417.2 2.5 pad_maximum_fusion
  422.0 51.7 %move.11 = (bf16[4,64,4224]{2,1,0:T(8,128)(2,1)}, bf16[2,4,128,1024]{3,2,1,0:T(8,128)(2,1)}) custom-call(bf16[4,64,4224]{2,1,0:T(8,128)(2,1)} %bitcast.99, bf16[4,2,128,1024]{3,2,1,0:T(8,128)(2,1)} %bitcast.91), custom_call_target="tpu_custom_call" | custom-call | flops 100000000 | bytes 8519680 | tf_op jit(solution)/shard_map/move/pallas_call | solution.py:871
  481.4 4.8 join.3
  487.1 2.7 fusion.4.refs_0_
  491.1 2.0 copy.263
  493.2 76.0 %attention_end.1 = (f32[128,2048]{1,0:T(8,128)}, bf16[4,64,1152]{2,1,0:T(8,128)(2,1)}, bf16[4,64,1024]{2,1,0:T(8,128)(2,1)}) custom-call(bf16[512,1664]{1,0:T(8,128)(2,1)} %fusion.4.refs_0_, bf16[512,2048]{1,0:T(8,128)(2,1)} %copy-done.22, f32[2048,128]{1,0:T(8,128)} %bitcast_add_fusion.refs_2_, bf16[128,2048]{1,0:T(8,128)(2,1)} %copy.242.refs_5_.refs_1_.refs_3_, ...), custom_call_target="tpu_custom_call" | custom-call | flops 100000000 | bytes 20447232 | tf_op jit(solution)/shard_map/attention_end/pallas_call | solution.py:1176
  572.3 3.8 join.2
  (205 shorter events, 62.0 us)
Async XLA Ops:
  7.2 173.1 %all-gather.3.cloned.1.call-start = ((), (), s32[]{:S(2)}) async-start(), calls=%async_computation.2 | async-start | bytes 2359296 | tf_op jit(solution)/shard_map/all_gather | solution.py:1288
  75.7 166.7 %all-gather.5.cloned.1.call-start = ((), (), s32[]{:S(2)}) async-start(), calls=%async_computation.3 | async-start | bytes 19464192 | tf_op jit(solution)/shard_map/all_gather | solution.py:1288
  76.9 3.6 copy-start.24
  80.4 5.7 copy-start.22
  144.0 275.8 %reduce-scatter.3.cloned.1.call-start = ((), (), s32[]{:S(2)}) async-start(), calls=%async_computation.4 | async-start | bytes 10813440 | tf_op jit(solution)/shard_map/reduce_scatter | solution.py:1284
  148.6 10.9 %copy-start.5 = (bf16[1024,256]{1,0:T(8,128)(2,1)}, bf16[1024,256]{1,0:T(8,128)(2,1)S(1)}, u32[]{:S(2)}) copy-start(bf16[1024,256]{1,0:T(8,128)(2,1)S(1)} %get-tuple-element.168.k_ref) | copy-start | bytes 1572868
  148.6 10.9 %copy-start.7 = (bf16[1024,256]{1,0:T(8,128)(2,1)}, bf16[1024,256]{1,0:T(8,128)(2,1)S(1)}, u32[]{:S(2)}) copy-start(bf16[1024,256]{1,0:T(8,128)(2,1)S(1)} %get-tuple-element.169.q_ref) | copy-start | bytes 1572868
  148.6 3.1 copy-start.11
  148.6 3.0 copy-start.13
  151.7 7.9 %copy-start.15 = (f32[1024,256]{1,0:T(8,128)}, f32[1024,256]{1,0:T(8,128)S(1)}, u32[]{:S(2)}) copy-start(f32[1024,256]{1,0:T(8,128)S(1)} %get-tuple-element.176.ld_ref) | copy-start | bytes 3145732
  180.3 3.7 copy-start
  327.1 164.0 %reduce-scatter.5.cloned.1.call-start = ((), (), s32[]{:S(2)}) async-start(), calls=%async_computation.5 | async-start | bytes 4718592 | tf_op jit(solution)/shard_map/reduce_scatter | solution.py:1284
  327.1 48.3 %copy-start.43 = (bf16[2048,512]{1,0:T(8,128)(2,1)S(1)}, bf16[2048,512]{1,0:T(8,128)(2,1)}, u32[]{:S(2)}) copy-start(bf16[2048,512]{1,0:T(8,128)(2,1)} %all-gather.3.cloned.1.call-done) | copy-start | bytes 6291460
  328.8 46.6 %copy-start.28 = (f32[512,1664]{1,0:T(8,128)S(1)}, f32[512,1664]{1,0:T(8,128)}, u32[]{:S(2)}) copy-start(f32[512,1664]{1,0:T(8,128)} %get-tuple-element.175) | copy-start | bytes 10223620
  330.2 45.3 %copy-start.20 = (f32[64,8,2,256]{3,1,2,0:T(8,128)S(1)}, f32[64,8,2,256]{3,1,2,0:T(8,128)}, u32[]{:S(2)}) copy-start(f32[64,8,2,256]{3,1,2,0:T(8,128)} %copy-done.19) | copy-start | bytes 3145732
  330.2 45.3 %copy-start.38 = (f32[512]{0:T(512)S(1)}, f32[512]{0:T(512)}, u32[]{:S(2)}) copy-start(f32[512]{0:T(512)} %copy-done.37) | copy-start | bytes 6148
  379.2 13.5 %copy-start.6 = (bf16[1024,256]{1,0:T(8,128)(2,1)S(1)}, bf16[1024,256]{1,0:T(8,128)(2,1)}, u32[]{:S(2)}) copy-start(bf16[1024,256]{1,0:T(8,128)(2,1)} %copy-done.5) | copy-start | bytes 1572868
  379.2 13.6 %copy-start.8 = (bf16[1024,256]{1,0:T(8,128)(2,1)S(1)}, bf16[1024,256]{1,0:T(8,128)(2,1)}, u32[]{:S(2)}) copy-start(bf16[1024,256]{1,0:T(8,128)(2,1)} %copy-done.7) | copy-start | bytes 1572868
  396.7 13.6 %copy-start.29 = (f32[1024,256]{1,0:T(8,128)S(1)}, f32[1024,256]{1,0:T(8,128)}, u32[]{:S(2)}) copy-start(f32[1024,256]{1,0:T(8,128)} %get-tuple-element.177) | copy-start | bytes 3145732
  493.1 78.4 %copy-start.39 = (bf16[64,16]{0,1:T(8,128)(2,1)S(1)}, bf16[64,16]{0,1:T(8,128)(2,1)}, u32[]{:S(2)}) copy-start(bf16[64,16]{0,1:T(8,128)(2,1)} %param.31) | copy-start | bytes 6148
  569.2 7.8 %copy-start.41 = (bf16[64]{0:T(256)(128)(2,1)S(1)}, bf16[64]{0:T(256)(128)(2,1)}, u32[]{:S(2)}) copy-start(bf16[64]{0:T(256)(128)(2,1)} %param.26) | copy-start | bytes 388
  569.2 7.8 %copy-start.42 = (bf16[64]{0:T(256)(128)(2,1)S(1)}, bf16[64]{0:T(256)(128)(2,1)}, u32[]{:S(2)}) copy-start(bf16[64]{0:T(256)(128)(2,1)} %param.36) | copy-start | bytes 388
  570.1 8.4 %copy-start.30 = (f32[128,2048]{1,0:T(8,128)S(1)}, f32[128,2048]{1,0:T(8,128)}, u32[]{:S(2)}) copy-start(f32[128,2048]{1,0:T(8,128)} %get-tuple-element.198) | copy-start | bytes 3145732
  571.6 7.8 %copy-start.36 = (f32[64,16]{0,1:T(8,128)}, f32[64,16]{0,1:T(8,128)S(1)}, u32[]{:S(2)}) copy-start(f32[64,16]{0,1:T(8,128)S(1)} %copy.271) | copy-start | bytes 12292
  (25 other events, 34.0 us)
Sparse Core Ops, SparseCore 0:
  75.8 38.3 all-gather.2
  144.1 98.1 all-gather.4
  327.2 91.9 reduce-scatter.2
  422.4 55.1 reduce-scatter.4
where the time goes:
time: 596 us; the launch traced here: 586 us
  Pallas kernels  473 us (79%)
  local copies, waits for them, and re-layouts  47.5 us (8%)
  other arithmetic  24.5 us (4%)
  matrix products  16.8 us (3%)
  between operations  15 us (3%)
  waiting for transfers between devices  9.58 us (2%)
    pallas_call x6, Pallas kernels, move(): pl.pallas_call(body, in_specs=in_specs, out_specs=out_specs, out_shape=sh...  221 us
    pallas_call x1, Pallas kernels, feed_forward(): pl.pallas_call(body, in_specs=[in_vmem, anywhere, anywhere], out_specs=[i...  84.7 us
    pallas_call x1, Pallas kernels, attention_end(): pl.pallas_call(body, in_specs=[in_vmem] * (3 + len(extras)) + [anywhere]...  76 us
    pallas_call x1, Pallas kernels, spread_and_gather(): pl.pallas_call(body, in_specs=[anywhere] * (parts + 2), out_specs=[anywhe...  60.7 us
    unnamed x104, local copies, waits for them, and re-layouts  20.9 us
    pallas_call x1, Pallas kernels, mix_backward(): pl.pallas_call(mix_backward_body, grid=(count,), in_specs=[tokens(DK), to...  13.6 us
  transfers between devices with their start and end apart: 4, of which 1 were waited for; matrix products, arithmetic and copies ran while one was open for 10% of the time, Pallas kernels for 42%

commit v1 on v0

--- a/solution.py
+++ b/solution.py
@@ -709,23 +709,24 @@
         return self.out_ref.at[self.place(index), :, pl.ds(sum(widths[:i]), widths[i])]
 
 
-def spread_and_gather(weights, block, other, sizes, number):
+def spread_and_gather(weights, block, others, sizes, number):
     X, C, Z, Y = sizes
     parts = len(weights)
     rows = weights[0].shape[0]
     total = sum(w.shape[1] // Z for w in weights[:-1]) + weights[-1].shape[1]
 
     def body(*refs):
-        w_refs, x_ref, o_ref = refs[:parts], refs[parts], refs[parts + 1]
-        spread_ref, out_ref, swapped_ref = refs[parts + 2 : parts + 5]
-        sems = refs[parts + 5 :]
+        extra = len(others)
+        w_refs, x_ref, o_refs = refs[:parts], refs[parts], refs[parts + 1 : parts + 1 + extra]
+        spread_ref, out_ref, swapped_ref = refs[parts + 1 + extra : parts + 4 + extra]
+        sems = refs[parts + 4 + extra :]
         x, c, _, y = (lax.axis_index(name) for name in OWN)
         first = FirstCuts(
             lambda index: ((x * C + c) * Y + y) * Z + index, Z, w_refs, spread_ref, *sems[:3]
         )
         spread = Spread(sizes, first, spread_ref, *sems[3:7])
         gather = Gather("z", Z, x_ref, out_ref, *sems[7:10])
-        swap = CutSwap("z", Z, [o_ref], swapped_ref, *sems[10:])
+        swap = CutSwap("z", Z, o_refs, swapped_ref, *sems[10:])
         greet(spread.peers())
         first.start()
         gather.start()
@@ -745,23 +746,23 @@
     anywhere = pl.BlockSpec(memory_space=pl.ANY)
     return pl.pallas_call(
         body,
-        in_specs=[anywhere] * (parts + 2),
+        in_specs=[anywhere] * (parts + 1 + len(others)),
         out_specs=[anywhere] * 3,
         out_shape=[
             jax.ShapeDtypeStruct((X * C * Y * Z, rows, total), BF),
             jax.ShapeDtypeStruct((Z * block.shape[0],) + block.shape[1:], block.dtype),
-            jax.ShapeDtypeStruct((Z, rows, other.shape[1] // Z), BF),
+            jax.ShapeDtypeStruct((Z, rows, sum(w.shape[1] for w in others) // Z), BF),
         ],
         scratch_shapes=CutSwap.scratch(Z, parts)
         + Spread.scratch(sizes)
         + Gather.scratch(Z)
-        + CutSwap.scratch(Z, 1),
+        + CutSwap.scratch(Z, len(others)),
         compiler_params=pltpu.CompilerParams(collective_id=number, has_side_effects=True),
         cost_estimate=pl.CostEstimate(
             flops=WAIT_FLOPS, bytes_accessed=rows * total * X * C * Y * Z * 2, transcendentals=0
         ),
         name="spread_and_gather",
-    )(*weights, block, other)
+    )(*weights, block, *others)
 
 
 def move(
@@ -884,25 +885,21 @@
     )(*values)
 
 
-def feed_forward(normed_own, mlp_piece, cotangent, number):
+def feed_forward(normed_own, mlp_piece, out_down, cotangent, number):
     count = lax.axis_size("z")
     own, width = normed_own.shape
-    group, ff = own * count, mlp_piece.shape[1] // 3
+    group, ff = own * count, mlp_piece.shape[1] // 2
     half = group // 2
     block = width // (2 * lax.axis_size("x"))
 
-    def body(x_ref, w_hbm, c_hbm, sum_ref, down_ref, grad_hbm,
+    def body(x_ref, w_hbm, d_hbm, c_hbm, sum_ref, down_ref, grad_hbm,
              w_ref, d_ref, c_ref, normed, hidden_grad, hidden, grads, partial, stage, received,
              load_sem, store_sem, pair_send, pair_arrive, gather_send, gather_arrive, local_sem, up, down, send, arrive):
         me, core = lax.axis_index("z"), lax.axis_index("c")
         loads = [
             pltpu.make_async_copy(source, target, load_sem.at[i])
             for i, (source, target) in enumerate(
-                [
-                    (c_hbm, c_ref),
-                    (w_hbm.at[:, pl.ds(2 * ff, ff)], d_ref),
-                    (w_hbm.at[:, pl.ds(0, 2 * ff)], w_ref),
-                ]
+                [(c_hbm, c_ref), (d_hbm.at[:, pl.ds(DV, ff)], d_ref), (w_hbm, w_ref)]
             )
         ]
         for load in loads:
@@ -1018,7 +1015,7 @@
     in_vmem, anywhere = pl.BlockSpec(memory_space=pltpu.VMEM), pl.BlockSpec(memory_space=pl.ANY)
     return pl.pallas_call(
         body,
-        in_specs=[in_vmem, anywhere, anywhere],
+        in_specs=[in_vmem, anywhere, anywhere, anywhere],
         out_specs=[in_vmem, in_vmem, anywhere],
         out_shape=[
             jax.ShapeDtypeStruct((own, width), F32),
@@ -1050,7 +1047,7 @@
             flops=WAIT_FLOPS, bytes_accessed=width * ff * 12, transcendentals=0
         ),
         name="feed_forward",
-    )(normed_own, mlp_piece, cotangent)
+    )(normed_own, mlp_piece, out_down, cotangent)
 
 
 def rows_of_core(block, number, by):
@@ -1298,7 +1295,7 @@
     own_tokens = blocked(tokens)
     input_weights, group_tokens, out_weights = spread_and_gather(
         [query_weight, key_weight, value_weight, gate_weight, small],
-        own_tokens, out_weight, (X, C, Z, Y), next(numbers),
+        own_tokens, [out_weight, down_weight], (X, C, Z, Y), next(numbers),
     )
     input_weights = input_weights.reshape(width, -1)
 
@@ -1346,10 +1343,11 @@
     values = jnp.swapaxes(low[:, 2 * DK : 2 * DK + DV].reshape(group, Y, dvp), 0, 1)
     sent = jnp.concatenate([jnp.broadcast_to(shared[None], (Y,) + shared.shape), values], axis=2)
     mlp_weights, sequence = move(
-        next(numbers), cuts=[([mlp_gate_weight, mlp_up_weight, down_weight], "z")],
+        next(numbers), cuts=[([mlp_gate_weight, mlp_up_weight], "z")],
         deals=[(sent.reshape(Y, Z, own, -1), "y", True)],
     )
-    out_piece = gather_rest(out_weights)
+    out_down = gather_rest(out_weights)
+    out_piece = out_down[:, :DV]
     mlp_piece = gather_rest(mlp_weights)
     sequence = sequence.reshape(total, -1)
     queries = sequence[:, :DK]
@@ -1391,7 +1389,7 @@
     hat_mid = residual * scale_mid
     normed_mlp = (hat_mid * mlp_gain_all).astype(BF)
     grad_normed_mlp, out_partial, mlp_partial = feed_forward(
-        normed_mlp, mlp_piece, group_cotangent, next(numbers)
+        normed_mlp, mlp_piece, out_down, group_cotangent, next(numbers)
     )
     mlp_sums = scatter_rest(mlp_partial, ("x", "y"))
 

time: 596 us -> 592 us (level)
  waiting for transfers between devices: 9.58 us -> 0.09 us
    pallas_call x2, Pallas kernels: 145 us -> 160 us  [the longest x1 89 us: feed_forward(): pl.pallas_call(body, in_specs=[in_vmem, anywhere, anywhere, anywhere], ou...]
    pallas_call x6, Pallas kernels: 221 us -> 211 us  [move(): pl.pallas_call(body, in_specs=in_specs, out_specs=out_specs, out_shape=sh...]
    all_gather x2, waiting for transfers between devices: 9.51 us -> 0.02 us  [gather_rest(): return lax.all_gather(value.reshape(Z * rows, -1), axes, axis=0, tiled=True)]
    unnamed x104 -> x102, local copies, waits for them, and re-layouts: 20.9 us -> 20.7 us
  transfers between devices with their start and end apart: 4 -> 4, of which waited for: 1 -> 0; matrix products, arithmetic and copies ran while one was open for 10% -> 11% of each run, Pallas kernels for 42% -> 41%
where the time goes in v1:
time: 592 us; the launch traced here: 583 us
  Pallas kernels  477 us (81%)
  local copies, waits for them, and re-layouts  47.3 us (8%)
  other arithmetic  24.5 us (4%)
  matrix products  19.4 us (3%)
  between operations  15 us (3%)
    pallas_call x6, Pallas kernels, move(): pl.pallas_call(body, in_specs=in_specs, out_specs=out_specs, out_shape=sh...  211 us
    pallas_call x1, Pallas kernels, feed_forward(): pl.pallas_call(body, in_specs=[in_vmem, anywhere, anywhere, anywhere], ou...  89 us
    pallas_call x1, Pallas kernels, attention_end(): pl.pallas_call(body, in_specs=[in_vmem] * (3 + len(extras)) + [anywhere]...  76.2 us
    pallas_call x1, Pallas kernels, spread_and_gather(): pl.pallas_call(body, in_specs=[anywhere] * (parts + 1 + len(others)), out...  70.6 us
    unnamed x102, local copies, waits for them, and re-layouts  20.7 us
    pallas_call x1, Pallas kernels, mix_backward(): pl.pallas_call(mix_backward_body, grid=(count,), in_specs=[tokens(DK), to...  13.6 us
  transfers between devices with their start and end apart: 4, of which 0 were waited for; matrix products, arithmetic and copies ran while one was open for 11% of the time, Pallas kernels for 41%

profile of v1, /device:TPU:9, one launch (start us, length us, event | category | flops | bytes accessed | tf_op | source)
XLA Modules:
  0.0 583.3 jit_solution(2650027527789290349)
XLA Ops:
  14.9 70.6 %spread_and_gather.1 = (bf16[32,64,1664]{2,1,0:T(8,128)(2,1)}, bf16[512,2048]{1,0:T(8,128)(2,1)}, bf16[4,64,1920]{2,1,0:T(8,128)(2,1)}) custom-call(bf16[64,1024]{1,0:T(8,128)(2,1)} %refs_2_.4, bf16[64,1024]{1,0:T(8,128)(2,1)} %refs_3_.3, bf16[64,2048]{1,0:T(8,128)(2,1)} %refs_4_.1, bf16[64,2048]{1,0:T(8,128)(2,1)} %refs_5_.1, bf16[64,128]{1,0:T(8,128)(2,1)} %pad.35.refs_4_, ...), custom_call_target="tpu_custom_call" | custom-call | flops 100000000 | bytes 6815744 | tf_op jit(solution)/shard_map/spread_and_gather/pallas_call | solution.py:747
  86.7 2.2 slice_reduce_fusion.1
  90.3 5.7 fusion.29
  98.7 46.0 %move.6 = (bf16[4,64,2816]{2,1,0:T(8,128)(2,1)}, bf16[4,2,128,896]{3,2,1,0:T(8,128)(2,1)}) custom-call(bf16[64,5632]{1,0:T(8,128)(2,1)} %refs_1_.5, bf16[64,5632]{1,0:T(8,128)(2,1)} %refs_2_.5, bf16[2,4,128,896]{3,2,1,0:T(8,128)(2,1)} %bitcast.93), custom_call_target="tpu_custom_call" | custom-call | flops 100000000 | bytes 6553600 | tf_op jit(solution)/shard_map/move/pallas_call | solution.py:872
  149.3 3.1 fusion.9
  152.4 7.9 %mix_forward.1 = (bf16[1024,256]{1,0:T(8,128)(2,1)S(1)}, bf16[8,256,256]{2,1,0:T(8,128)(2,1)S(1)}, bf16[8,128,128]{2,1,0:T(8,128)(2,1)S(1)}) custom-call(bf16[1024,256]{1,0:T(8,128)(2,1)S(1)} %get-tuple-element.169.q_ref, bf16[1024,256]{1,0:T(8,128)(2,1)S(1)} %get-tuple-element.168.k_ref, bf16[1024,256]{1,0:T(8,128)(2,1)S(1)} %get-tuple-element.167.v_ref, ...), custom_call_target="tpu_custom_call" | custom-call | flops 2080374784 | bytes 4194304 | tf_op jit(solution)/shard_map/mix_forward/pallas_call | solution.py:204
  162.7 11.2 %move.7 = bf16[2,4,128,256]{3,2,1,0:T(8,128)(2,1)} custom-call(bf16[4,2,128,256]{3,2,1,0:T(8,128)(2,1)} %bitcast.83), custom_call_target="tpu_custom_call" | custom-call | flops 100000000 | bytes 1048576 | tf_op jit(solution)/shard_map/move/pallas_call | solution.py:872
  179.0 2.9 convolution_convert_fusion.2.refs_0_
  181.9 45.3 %move.8 = (f32[128,2048]{1,0:T(8,128)S(1)}, bf16[512,2048]{1,0:T(8,128)(2,1)S(1)}) custom-call(bf16[512,2048]{1,0:T(8,128)(2,1)S(1)} %convolution_convert_fusion.2.refs_0_, bf16[128,2048]{1,0:T(8,128)(2,1)S(1)} %copy-done, bf16[128,2048]{1,0:T(8,128)(2,1)S(1)} %copy.253.refs_2_), custom_call_target="tpu_custom_call" | custom-call | flops 100000000 | bytes 6291456 | tf_op jit(solution)/shard_map/move/pallas_call | solution.py:872
  229.7 89.0 %feed_forward.1 = (f32[128,2048]{1,0:T(8,128)}, bf16[512,2048]{1,0:T(8,128)(2,1)}, bf16[1024,4224]{1,0:T(8,128)(2,1)}) custom-call(bf16[128,2048]{1,0:T(8,128)(2,1)} %multiply_convert_fusion.3.x_ref, bf16[2048,2816]{1,0:T(8,128)(2,1)} %all-gather.5.cloned.1.call-done.w_hbm, bf16[2048,1920]{1,0:T(8,128)(2,1)} %all-gather.3.cloned.1.call-done.d_hbm, ...), custom_call_target="tpu_custom_call" | custom-call | flops 100000000 | bytes 34603008 | tf_op jit(solution)/shard_map/feed_forward/pallas_call | solution.py:1016
  322.4 45.3 %move.9 = (f32[128,2048]{1,0:T(8,128)S(1)}, bf16[512,2048]{1,0:T(8,128)(2,1)S(1)}) custom-call(bf16[512,2048]{1,0:T(8,128)(2,1)S(1)} %copy-done.1, f32[128,2048]{1,0:T(8,128)S(1)} %get-tuple-element.58.refs_1_, bf16[128,2048]{1,0:T(8,128)(2,1)S(1)} %get-tuple-element.163.refs_2_), custom_call_target="tpu_custom_call" | custom-call | flops 100000000 | bytes 6291456 | tf_op jit(solution)/shard_map/move/pallas_call | solution.py:872
  367.7 4.5 multiply_reduce_fusion
  373.9 2.1 reshape.290
  376.0 1.9 copy.256
  377.9 11.4 %move.10 = bf16[4,2,128,256]{3,2,1,0:T(8,128)(2,1)} custom-call(bf16[2,4,128,256]{3,2,1,0:T(8,128)(2,1)} %bitcast.105), custom_call_target="tpu_custom_call" | custom-call | flops 100000000 | bytes 1048576 | tf_op jit(solution)/shard_map/move/pallas_call | solution.py:872
  393.1 13.6 %mix_backward.1 = (bf16[1024,256]{1,0:T(8,128)(2,1)S(1)}, bf16[1024,256]{1,0:T(8,128)(2,1)S(1)}, bf16[1024,256]{1,0:T(8,128)(2,1)S(1)}, f32[1024,256]{1,0:T(8,128)}) custom-call(bf16[1024,256]{1,0:T(8,128)(2,1)S(1)} %copy-done.8, bf16[1024,256]{1,0:T(8,128)(2,1)S(1)} %copy-done.6, bf16[1024,256]{1,0:T(8,128)(2,1)S(1)} %get-tuple-element.167.v_ref, ...), custom_call_target="tpu_custom_call" | custom-call | flops 3959422976 | bytes 6291456 | tf_op jit(solution)/shard_map/mix_backward/pallas_call | solution.py:234
  413.7 2.6 pad_maximum_fusion
  418.6 51.8 %move.11 = (bf16[4,64,4224]{2,1,0:T(8,128)(2,1)}, bf16[2,4,128,1024]{3,2,1,0:T(8,128)(2,1)}) custom-call(bf16[4,64,4224]{2,1,0:T(8,128)(2,1)} %bitcast.96, bf16[4,2,128,1024]{3,2,1,0:T(8,128)(2,1)} %bitcast.89), custom_call_target="tpu_custom_call" | custom-call | flops 100000000 | bytes 8519680 | tf_op jit(solution)/shard_map/move/pallas_call | solution.py:872
  471.5 1.7 slice_reduce_fusion
  478.1 4.8 join.3
  483.8 2.7 fusion.7.refs_0_
  487.7 2.0 copy.263
  489.8 76.2 %attention_end.1 = (f32[128,2048]{1,0:T(8,128)}, bf16[4,64,1152]{2,1,0:T(8,128)(2,1)}, bf16[4,64,1024]{2,1,0:T(8,128)(2,1)}) custom-call(bf16[512,1664]{1,0:T(8,128)(2,1)} %fusion.7.refs_0_, bf16[512,2048]{1,0:T(8,128)(2,1)} %copy-done.22, f32[2048,128]{1,0:T(8,128)} %bitcast_add_fusion.refs_2_, bf16[128,2048]{1,0:T(8,128)(2,1)} %copy.242.refs_5_.refs_1_.refs_3_, ...), custom_call_target="tpu_custom_call" | custom-call | flops 100000000 | bytes 20447232 | tf_op jit(solution)/shard_map/attention_end/pallas_call | solution.py:1173
  569.2 3.8 join.2
  (203 shorter events, 60.1 us)
Async XLA Ops:
  7.2 171.1 %all-gather.3.cloned.1.call-start = ((), (), s32[]{:S(2)}) async-start(), calls=%async_computation.2 | async-start | bytes 8847360 | tf_op jit(solution)/shard_map/all_gather | solution.py:1285
  85.6 144.2 %all-gather.5.cloned.1.call-start = ((), (), s32[]{:S(2)}) async-start(), calls=%async_computation.3 | async-start | bytes 12976128 | tf_op jit(solution)/shard_map/all_gather | solution.py:1285
  86.7 3.6 copy-start.24
  90.3 5.7 copy-start.22
  98.7 46.5 %copy-start.43 = (s32[1,8]{1,0:T(1,128)S(1)}, s32[1,8]{1,0:T(1,128)}, u32[]{:S(2)}) copy-start(s32[1,8]{1,0:T(1,128)} %param.24) | copy-start | bytes 100
  144.8 271.5 %reduce-scatter.3.cloned.1.call-start = ((), (), s32[]{:S(2)}) async-start(), calls=%async_computation.4 | async-start | bytes 10813440 | tf_op jit(solution)/shard_map/reduce_scatter | solution.py:1281
  149.3 11.0 %copy-start.5 = (bf16[1024,256]{1,0:T(8,128)(2,1)}, bf16[1024,256]{1,0:T(8,128)(2,1)S(1)}, u32[]{:S(2)}) copy-start(bf16[1024,256]{1,0:T(8,128)(2,1)S(1)} %get-tuple-element.168.k_ref) | copy-start | bytes 1572868
  149.3 11.0 %copy-start.7 = (bf16[1024,256]{1,0:T(8,128)(2,1)}, bf16[1024,256]{1,0:T(8,128)(2,1)S(1)}, u32[]{:S(2)}) copy-start(bf16[1024,256]{1,0:T(8,128)(2,1)S(1)} %get-tuple-element.169.q_ref) | copy-start | bytes 1572868
  149.3 3.1 copy-start.11
  152.4 7.9 %copy-start.15 = (f32[1024,256]{1,0:T(8,128)}, f32[1024,256]{1,0:T(8,128)S(1)}, u32[]{:S(2)}) copy-start(f32[1024,256]{1,0:T(8,128)S(1)} %get-tuple-element.176.ld_ref) | copy-start | bytes 3145732
  178.2 3.7 copy-start
  318.7 169.0 %reduce-scatter.5.cloned.1.call-start = ((), (), s32[]{:S(2)}) async-start(), calls=%async_computation.5 | async-start | bytes 4718592 | tf_op jit(solution)/shard_map/reduce_scatter | solution.py:1281
  320.4 47.3 %copy-start.28 = (f32[512,1664]{1,0:T(8,128)S(1)}, f32[512,1664]{1,0:T(8,128)}, u32[]{:S(2)}) copy-start(f32[512,1664]{1,0:T(8,128)} %get-tuple-element.175) | copy-start | bytes 10223620
  321.8 46.0 %copy-start.20 = (f32[64,8,2,256]{3,1,2,0:T(8,128)S(1)}, f32[64,8,2,256]{3,1,2,0:T(8,128)}, u32[]{:S(2)}) copy-start(f32[64,8,2,256]{3,1,2,0:T(8,128)} %copy-done.19) | copy-start | bytes 3145732
  321.8 46.0 %copy-start.38 = (f32[512]{0:T(512)S(1)}, f32[512]{0:T(512)}, u32[]{:S(2)}) copy-start(f32[512]{0:T(512)} %copy-done.37) | copy-start | bytes 6148
  367.7 4.6 copy-start.9
  373.9 15.3 %copy-start.6 = (bf16[1024,256]{1,0:T(8,128)(2,1)S(1)}, bf16[1024,256]{1,0:T(8,128)(2,1)}, u32[]{:S(2)}) copy-start(bf16[1024,256]{1,0:T(8,128)(2,1)} %copy-done.5) | copy-start | bytes 1572868
  373.9 15.3 %copy-start.8 = (bf16[1024,256]{1,0:T(8,128)(2,1)S(1)}, bf16[1024,256]{1,0:T(8,128)(2,1)}, u32[]{:S(2)}) copy-start(bf16[1024,256]{1,0:T(8,128)(2,1)} %copy-done.7) | copy-start | bytes 1572868
  393.1 13.6 %copy-start.29 = (f32[1024,256]{1,0:T(8,128)S(1)}, f32[1024,256]{1,0:T(8,128)}, u32[]{:S(2)}) copy-start(f32[1024,256]{1,0:T(8,128)} %get-tuple-element.177) | copy-start | bytes 3145732
  489.8 78.7 %copy-start.39 = (bf16[64,16]{0,1:T(8,128)(2,1)S(1)}, bf16[64,16]{0,1:T(8,128)(2,1)}, u32[]{:S(2)}) copy-start(bf16[64,16]{0,1:T(8,128)(2,1)} %param.31) | copy-start | bytes 6148
  566.0 7.8 %copy-start.41 = (bf16[64]{0:T(256)(128)(2,1)S(1)}, bf16[64]{0:T(256)(128)(2,1)}, u32[]{:S(2)}) copy-start(bf16[64]{0:T(256)(128)(2,1)} %param.26) | copy-start | bytes 388
  566.0 7.8 %copy-start.42 = (bf16[64]{0:T(256)(128)(2,1)S(1)}, bf16[64]{0:T(256)(128)(2,1)}, u32[]{:S(2)}) copy-start(bf16[64]{0:T(256)(128)(2,1)} %param.36) | copy-start | bytes 388
  566.9 8.4 %copy-start.30 = (f32[128,2048]{1,0:T(8,128)S(1)}, f32[128,2048]{1,0:T(8,128)}, u32[]{:S(2)}) copy-start(f32[128,2048]{1,0:T(8,128)} %get-tuple-element.198) | copy-start | bytes 3145732
  568.5 7.8 %copy-start.36 = (f32[64,16]{0,1:T(8,128)}, f32[64,16]{0,1:T(8,128)S(1)}, u32[]{:S(2)}) copy-start(f32[64,16]{0,1:T(8,128)S(1)} %copy.271) | copy-start | bytes 12292
  (24 other events, 34.0 us)
Sparse Core Ops, SparseCore 0:
  85.7 68.3 all-gather.2
  156.0 72.1 all-gather.4
  318.8 94.4 reduce-scatter.2
  416.5 57.6 reduce-scatter.4

commit v2 on v1

--- a/solution.py
+++ b/solution.py
@@ -999,7 +999,7 @@
         scatter.start([2])
         units = list(range(width // TILE))
         stages = [(step, far) for step in range(count - 1) for far in (False, True)]
-        spare = len(units) - len(stages)
+        spare = len(units) - len(stages) + 2
         for i in units[: max(spare, 0)]:
             weight_rows(i)
         rest = units[max(spare, 0) :]

time: 592 us -> 589 us (level)
  no operation moved by 1% of the time
where the time goes in v2:
time: 589 us; the launch traced here: 579 us
  Pallas kernels  472 us (80%)
  local copies, waits for them, and re-layouts  47.5 us (8%)
  other arithmetic  24.4 us (4%)
  matrix products  19.5 us (3%)
  between operations  15 us (3%)
    pallas_call x6, Pallas kernels, move(): pl.pallas_call(body, in_specs=in_specs, out_specs=out_specs, out_shape=sh...  212 us
    pallas_call x1, Pallas kernels, feed_forward(): pl.pallas_call(body, in_specs=[in_vmem, anywhere, anywhere, anywhere], ou...  83.7 us
    pallas_call x1, Pallas kernels, attention_end(): pl.pallas_call(body, in_specs=[in_vmem] * (3 + len(extras)) + [anywhere]...  76.3 us
    pallas_call x1, Pallas kernels, spread_and_gather(): pl.pallas_call(body, in_specs=[anywhere] * (parts + 1 + len(others)), out...  70.6 us
    unnamed x102, local copies, waits for them, and re-layouts  20.9 us
    pallas_call x1, Pallas kernels, mix_backward(): pl.pallas_call(mix_backward_body, grid=(count,), in_specs=[tokens(DK), to...  13.6 us
  transfers between devices with their start and end apart: 4, of which 0 were waited for; matrix products, arithmetic and copies ran while one was open for 11% of the time, Pallas kernels for 41%

profile of v2, /device:TPU:9, one launch (start us, length us, event | category | flops | bytes accessed | tf_op | source)
XLA Modules:
  0.0 579.1 jit_solution(5576820258456831339)
XLA Ops:
  14.9 70.6 %spread_and_gather.1 = (bf16[32,64,1664]{2,1,0:T(8,128)(2,1)}, bf16[512,2048]{1,0:T(8,128)(2,1)}, bf16[4,64,1920]{2,1,0:T(8,128)(2,1)}) custom-call(bf16[64,1024]{1,0:T(8,128)(2,1)} %refs_2_.4, bf16[64,1024]{1,0:T(8,128)(2,1)} %refs_3_.3, bf16[64,2048]{1,0:T(8,128)(2,1)} %refs_4_.1, bf16[64,2048]{1,0:T(8,128)(2,1)} %refs_5_.1, bf16[64,128]{1,0:T(8,128)(2,1)} %pad.35.refs_4_, ...), custom_call_target="tpu_custom_call" | custom-call | flops 100000000 | bytes 6815744 | tf_op jit(solution)/shard_map/spread_and_gather/pallas_call | solution.py:747
  86.7 2.2 slice_reduce_fusion.1
  90.3 5.7 fusion.29
  98.7 46.0 %move.6 = (bf16[4,64,2816]{2,1,0:T(8,128)(2,1)}, bf16[4,2,128,896]{3,2,1,0:T(8,128)(2,1)}) custom-call(bf16[64,5632]{1,0:T(8,128)(2,1)} %refs_1_.5, bf16[64,5632]{1,0:T(8,128)(2,1)} %refs_2_.5, bf16[2,4,128,896]{3,2,1,0:T(8,128)(2,1)} %bitcast.93), custom_call_target="tpu_custom_call" | custom-call | flops 100000000 | bytes 6553600 | tf_op jit(solution)/shard_map/move/pallas_call | solution.py:872
  149.3 3.1 fusion.9
  152.4 7.9 %mix_forward.1 = (bf16[1024,256]{1,0:T(8,128)(2,1)S(1)}, bf16[8,256,256]{2,1,0:T(8,128)(2,1)S(1)}, bf16[8,128,128]{2,1,0:T(8,128)(2,1)S(1)}) custom-call(bf16[1024,256]{1,0:T(8,128)(2,1)S(1)} %get-tuple-element.169.q_ref, bf16[1024,256]{1,0:T(8,128)(2,1)S(1)} %get-tuple-element.168.k_ref, bf16[1024,256]{1,0:T(8,128)(2,1)S(1)} %get-tuple-element.167.v_ref, ...), custom_call_target="tpu_custom_call" | custom-call | flops 2080374784 | bytes 4194304 | tf_op jit(solution)/shard_map/mix_forward/pallas_call | solution.py:204
  162.7 11.2 %move.7 = bf16[2,4,128,256]{3,2,1,0:T(8,128)(2,1)} custom-call(bf16[4,2,128,256]{3,2,1,0:T(8,128)(2,1)} %bitcast.83), custom_call_target="tpu_custom_call" | custom-call | flops 100000000 | bytes 1048576 | tf_op jit(solution)/shard_map/move/pallas_call | solution.py:872
  179.0 2.9 convolution_convert_fusion.2.refs_0_
  181.9 45.3 %move.8 = (f32[128,2048]{1,0:T(8,128)S(1)}, bf16[512,2048]{1,0:T(8,128)(2,1)S(1)}) custom-call(bf16[512,2048]{1,0:T(8,128)(2,1)S(1)} %convolution_convert_fusion.2.refs_0_, bf16[128,2048]{1,0:T(8,128)(2,1)S(1)} %copy-done, bf16[128,2048]{1,0:T(8,128)(2,1)S(1)} %copy.253.refs_2_), custom_call_target="tpu_custom_call" | custom-call | flops 100000000 | bytes 6291456 | tf_op jit(solution)/shard_map/move/pallas_call | solution.py:872
  229.7 83.7 %feed_forward.1 = (f32[128,2048]{1,0:T(8,128)}, bf16[512,2048]{1,0:T(8,128)(2,1)}, bf16[1024,4224]{1,0:T(8,128)(2,1)}) custom-call(bf16[128,2048]{1,0:T(8,128)(2,1)} %multiply_convert_fusion.3.x_ref, bf16[2048,2816]{1,0:T(8,128)(2,1)} %all-gather.5.cloned.1.call-done.w_hbm, bf16[2048,1920]{1,0:T(8,128)(2,1)} %all-gather.3.cloned.1.call-done.d_hbm, ...), custom_call_target="tpu_custom_call" | custom-call | flops 100000000 | bytes 34603008 | tf_op jit(solution)/shard_map/feed_forward/pallas_call | solution.py:1016
  317.1 45.0 %move.9 = (f32[128,2048]{1,0:T(8,128)S(1)}, bf16[512,2048]{1,0:T(8,128)(2,1)S(1)}) custom-call(bf16[512,2048]{1,0:T(8,128)(2,1)S(1)} %copy-done.1, f32[128,2048]{1,0:T(8,128)S(1)} %get-tuple-element.58.refs_1_, bf16[128,2048]{1,0:T(8,128)(2,1)S(1)} %get-tuple-element.163.refs_2_), custom_call_target="tpu_custom_call" | custom-call | flops 100000000 | bytes 6291456 | tf_op jit(solution)/shard_map/move/pallas_call | solution.py:872
  362.1 4.6 multiply_reduce_fusion
  368.3 2.1 reshape.290
  370.4 1.9 copy.256
  372.3 14.9 %move.10 = bf16[4,2,128,256]{3,2,1,0:T(8,128)(2,1)} custom-call(bf16[2,4,128,256]{3,2,1,0:T(8,128)(2,1)} %bitcast.105), custom_call_target="tpu_custom_call" | custom-call | flops 100000000 | bytes 1048576 | tf_op jit(solution)/shard_map/move/pallas_call | solution.py:872
  391.1 13.6 %mix_backward.1 = (bf16[1024,256]{1,0:T(8,128)(2,1)S(1)}, bf16[1024,256]{1,0:T(8,128)(2,1)S(1)}, bf16[1024,256]{1,0:T(8,128)(2,1)S(1)}, f32[1024,256]{1,0:T(8,128)}) custom-call(bf16[1024,256]{1,0:T(8,128)(2,1)S(1)} %copy-done.8, bf16[1024,256]{1,0:T(8,128)(2,1)S(1)} %copy-done.6, bf16[1024,256]{1,0:T(8,128)(2,1)S(1)} %get-tuple-element.167.v_ref, ...), custom_call_target="tpu_custom_call" | custom-call | flops 3959422976 | bytes 6291456 | tf_op jit(solution)/shard_map/mix_backward/pallas_call | solution.py:234
  411.8 2.6 pad_maximum_fusion
  416.7 49.5 %move.11 = (bf16[4,64,4224]{2,1,0:T(8,128)(2,1)}, bf16[2,4,128,1024]{3,2,1,0:T(8,128)(2,1)}) custom-call(bf16[4,64,4224]{2,1,0:T(8,128)(2,1)} %bitcast.96, bf16[4,2,128,1024]{3,2,1,0:T(8,128)(2,1)} %bitcast.89), custom_call_target="tpu_custom_call" | custom-call | flops 100000000 | bytes 8519680 | tf_op jit(solution)/shard_map/move/pallas_call | solution.py:872
  467.2 1.7 slice_reduce_fusion
  473.9 4.8 join.3
  479.5 2.7 fusion.7.refs_0_
  483.5 2.0 copy.263
  485.6 76.3 %attention_end.1 = (f32[128,2048]{1,0:T(8,128)}, bf16[4,64,1152]{2,1,0:T(8,128)(2,1)}, bf16[4,64,1024]{2,1,0:T(8,128)(2,1)}) custom-call(bf16[512,1664]{1,0:T(8,128)(2,1)} %fusion.7.refs_0_, bf16[512,2048]{1,0:T(8,128)(2,1)} %copy-done.22, f32[2048,128]{1,0:T(8,128)} %bitcast_add_fusion.refs_2_, bf16[128,2048]{1,0:T(8,128)(2,1)} %copy.242.refs_5_.refs_1_.refs_3_, ...), custom_call_target="tpu_custom_call" | custom-call | flops 100000000 | bytes 20447232 | tf_op jit(solution)/shard_map/attention_end/pallas_call | solution.py:1173
  565.0 3.8 join.2
  (203 shorter events, 60.2 us)
Async XLA Ops:
  7.2 171.1 %all-gather.3.cloned.1.call-start = ((), (), s32[]{:S(2)}) async-start(), calls=%async_computation.2 | async-start | bytes 8847360 | tf_op jit(solution)/shard_map/all_gather | solution.py:1285
  85.6 144.2 %all-gather.5.cloned.1.call-start = ((), (), s32[]{:S(2)}) async-start(), calls=%async_computation.3 | async-start | bytes 12976128 | tf_op jit(solution)/shard_map/all_gather | solution.py:1285
  86.7 3.6 copy-start.24
  90.3 5.7 copy-start.22
  98.7 46.5 %copy-start.43 = (s32[1,8]{1,0:T(1,128)S(1)}, s32[1,8]{1,0:T(1,128)}, u32[]{:S(2)}) copy-start(s32[1,8]{1,0:T(1,128)} %param.24) | copy-start | bytes 100
  144.8 269.6 %reduce-scatter.3.cloned.1.call-start = ((), (), s32[]{:S(2)}) async-start(), calls=%async_computation.4 | async-start | bytes 10813440 | tf_op jit(solution)/shard_map/reduce_scatter | solution.py:1281
  149.3 11.0 %copy-start.5 = (bf16[1024,256]{1,0:T(8,128)(2,1)}, bf16[1024,256]{1,0:T(8,128)(2,1)S(1)}, u32[]{:S(2)}) copy-start(bf16[1024,256]{1,0:T(8,128)(2,1)S(1)} %get-tuple-element.168.k_ref) | copy-start | bytes 1572868
  149.3 11.0 %copy-start.7 = (bf16[1024,256]{1,0:T(8,128)(2,1)}, bf16[1024,256]{1,0:T(8,128)(2,1)S(1)}, u32[]{:S(2)}) copy-start(bf16[1024,256]{1,0:T(8,128)(2,1)S(1)} %get-tuple-element.169.q_ref) | copy-start | bytes 1572868
  149.3 3.1 copy-start.11
  152.4 7.9 %copy-start.15 = (f32[1024,256]{1,0:T(8,128)}, f32[1024,256]{1,0:T(8,128)S(1)}, u32[]{:S(2)}) copy-start(f32[1024,256]{1,0:T(8,128)S(1)} %get-tuple-element.176.ld_ref) | copy-start | bytes 3145732
  178.2 3.7 copy-start
  313.4 170.1 %reduce-scatter.5.cloned.1.call-start = ((), (), s32[]{:S(2)}) async-start(), calls=%async_computation.5 | async-start | bytes 4718592 | tf_op jit(solution)/shard_map/reduce_scatter | solution.py:1281
  315.1 46.9 %copy-start.28 = (f32[512,1664]{1,0:T(8,128)S(1)}, f32[512,1664]{1,0:T(8,128)}, u32[]{:S(2)}) copy-start(f32[512,1664]{1,0:T(8,128)} %get-tuple-element.175) | copy-start | bytes 10223620
  316.4 45.6 %copy-start.20 = (f32[64,8,2,256]{3,1,2,0:T(8,128)S(1)}, f32[64,8,2,256]{3,1,2,0:T(8,128)}, u32[]{:S(2)}) copy-start(f32[64,8,2,256]{3,1,2,0:T(8,128)} %copy-done.19) | copy-start | bytes 3145732
  316.4 45.6 %copy-start.38 = (f32[512]{0:T(512)S(1)}, f32[512]{0:T(512)}, u32[]{:S(2)}) copy-start(f32[512]{0:T(512)} %copy-done.37) | copy-start | bytes 6148
  362.0 4.7 copy-start.9
  368.3 18.9 %copy-start.6 = (bf16[1024,256]{1,0:T(8,128)(2,1)S(1)}, bf16[1024,256]{1,0:T(8,128)(2,1)}, u32[]{:S(2)}) copy-start(bf16[1024,256]{1,0:T(8,128)(2,1)} %copy-done.5) | copy-start | bytes 1572868
  368.3 18.9 %copy-start.8 = (bf16[1024,256]{1,0:T(8,128)(2,1)S(1)}, bf16[1024,256]{1,0:T(8,128)(2,1)}, u32[]{:S(2)}) copy-start(bf16[1024,256]{1,0:T(8,128)(2,1)} %copy-done.7) | copy-start | bytes 1572868
  391.1 13.6 %copy-start.29 = (f32[1024,256]{1,0:T(8,128)S(1)}, f32[1024,256]{1,0:T(8,128)}, u32[]{:S(2)}) copy-start(f32[1024,256]{1,0:T(8,128)} %get-tuple-element.177) | copy-start | bytes 3145732
  485.6 78.7 %copy-start.39 = (bf16[64,16]{0,1:T(8,128)(2,1)S(1)}, bf16[64,16]{0,1:T(8,128)(2,1)}, u32[]{:S(2)}) copy-start(bf16[64,16]{0,1:T(8,128)(2,1)} %param.31) | copy-start | bytes 6148
  561.9 7.8 %copy-start.41 = (bf16[64]{0:T(256)(128)(2,1)S(1)}, bf16[64]{0:T(256)(128)(2,1)}, u32[]{:S(2)}) copy-start(bf16[64]{0:T(256)(128)(2,1)} %param.26) | copy-start | bytes 388
  561.9 7.8 %copy-start.42 = (bf16[64]{0:T(256)(128)(2,1)S(1)}, bf16[64]{0:T(256)(128)(2,1)}, u32[]{:S(2)}) copy-start(bf16[64]{0:T(256)(128)(2,1)} %param.36) | copy-start | bytes 388
  562.8 8.4 %copy-start.30 = (f32[128,2048]{1,0:T(8,128)S(1)}, f32[128,2048]{1,0:T(8,128)}, u32[]{:S(2)}) copy-start(f32[128,2048]{1,0:T(8,128)} %get-tuple-element.198) | copy-start | bytes 3145732
  564.3 7.8 %copy-start.36 = (f32[64,16]{0,1:T(8,128)}, f32[64,16]{0,1:T(8,128)S(1)}, u32[]{:S(2)}) copy-start(f32[64,16]{0,1:T(8,128)S(1)} %copy.271) | copy-start | bytes 12292
  (24 other events, 34.2 us)
Sparse Core Ops, SparseCore 0:
  85.7 68.3 all-gather.2
  156.0 72.1 all-gather.4
  313.5 96.2 reduce-scatter.2
  414.5 55.9 reduce-scatter.4
